TPU v7x, 32 devices: a whole 2x2x4 slice. The times are simulated.
32 devices in a mesh: expert: 8 (over z, x), tensor: 4 (over y, core).
Axes of the slice: x: 2, y: 2, z: 4, core: 2. Of those that a mesh axis runs over, the one named last changes fastest.
Arguments:
- tokens: bfloat16 [4096, 768], P('expert'), may hold values from -6 to 6
- cotangent: bfloat16 [4096, 768], P('expert', 'tensor'), may hold values from -6 to 6
- norm1_gain: float32 [768], replicated, may hold values from 0.5 to 1.5
- w_query: bfloat16 [768, 768], P(None, 'tensor'), may hold values from -0.21875 to 0.21875
- w_key: bfloat16 [768, 768], P(None, 'tensor'), may hold values from -0.21875 to 0.21875
- w_value: bfloat16 [768, 768], P(None, 'tensor'), may hold values from -0.21875 to 0.21875
- w_attn_out: bfloat16 [768, 768], P('tensor'), may hold values from -2.5 to 2.5
- bias_table: float32 [32, 12], P(None, 'tensor'), may hold values from -3 to 3
- norm2_gain: float32 [768], P('tensor'), may hold values from 0.5 to 1.5
- w_router: bfloat16 [768, 8], P('tensor'), may hold values from -0.15625 to 0.15625
- expert_in: bfloat16 [8, 768, 3072], P('expert', None, 'tensor'), may hold values from -0.21875 to 0.21875
- expert_out: bfloat16 [8, 3072, 768], P('expert', 'tensor'), may hold values from -1.25 to 1.25
- route: int32 [4096], P('expert'), may hold values from 0 to 7, as said below
- slot: int32 [4096], P('expert'), may hold values from 0 to 127, as said below
- segment: int32 [4096], P('expert'), may hold values from 0 to 15, never falling along the last dimension, each value on 1 to 512 neighbouring positions
- rel_bucket: int32 [1023], replicated, may hold values from 0 to 31, as said below
Outputs:
- block_out: bfloat16 [4096, 768], P('expert', 'tensor')
- input_grad: float32 [4096, 768], P('expert', 'tensor')
- norm1_gain_grad: float32 [768], replicated
- query_grad: float32 [768, 768], P(None, 'tensor')
- key_grad: float32 [768, 768], P(None, 'tensor')
- value_grad: float32 [768, 768], P(None, 'tensor')
- attn_out_grad: float32 [768, 768], P('tensor')
- table_grad: float32 [32, 12], P(None, 'tensor')
- norm2_gain_grad: float32 [768], P('tensor')
- router_grad: float32 [768, 8], P('tensor')
- expert_in_grad: float32 [8, 768, 3072], P('expert', None, 'tensor')
- expert_out_grad: float32 [8, 3072, 768], P('expert', 'tensor')
Inputs may be any that keep to these rules, and one draw needn't show every extreme that they name: `route`: in each aligned block of 512 rows no expert is named more than 128 times, and one expert, the same in every block, is named exactly 128 times in every block. Within each aligned block of 512 rows no two tokens share both route and slot. `segment`: never falls along the tokens; a document holds 1 to 512 tokens. `rel_bucket`: entry 511 + r belongs to a key r positions after its query; it grows with the distance on each side, offsets after the query take buckets above 16 and offset 0 takes bucket 0.
All inputs are finite; a program needn't handle non-finite values.
Results may differ from a plain program's by a relative error of at most 0.015.
Values may be sent and summed in bfloat16 or wider, within the bound.
No kernel may reach another device: no remote copies, remote signals or barrier semaphores. Data moves between devices by JAX's collectives and lax.ppermute only.
A program may use at most 128 MiB of HBM per device.

v0:
```python
import functools

import jax
import jax.numpy as jnp
from jax import lax
from jax.experimental import pallas as pl
from jax.experimental.pallas import tpu as pltpu
from jax.sharding import PartitionSpec as P

HDIM = 64
EPSILON = 1e-06
MASKED_SCORE = -1e30
SCORE_SCALE = 0.125
PRECISE = lax.Precision.HIGHEST
F32 = jnp.float32
BF16 = jnp.bfloat16
GELU_C = 0.7978845608028654
GELU_A = 0.044715
CHUNK = 128
GROUPS = 1


def dot_nn(a, b, precision=None):
    return lax.dot_general(
        a, b, (((1,), (0,)), ((), ())), precision=precision, preferred_element_type=F32
    )


def dot_nt(a, b, precision=None):
    return lax.dot_general(
        a, b, (((1,), (1,)), ((), ())), precision=precision, preferred_element_type=F32
    )


def dot_tn(a, b, precision=None):
    return lax.dot_general(
        a, b, (((0,), (0,)), ((), ())), precision=precision, preferred_element_type=F32
    )


def row_scale(rows):
    return lax.rsqrt(jnp.mean(rows * rows, axis=1, keepdims=True) + EPSILON)


def bucket_marks(bucket, count):
    width = bucket.shape[0]
    return lax.broadcasted_iota(jnp.int32, (count, width), 0) == bucket[...].reshape(1, width)


def in_order(blocks, rank, place, axis):
    for j, block in enumerate(blocks):
        place[rank ^ j] = block[...]
    return jnp.concatenate([place[r] for r in range(len(blocks))], axis=axis)


def as_column(row):
    return jnp.broadcast_to(row, (128, row.shape[1])).T[:, 0:1]


def softmax_rows(logits):
    shifted = jnp.exp(logits - jnp.max(logits, axis=1, keepdims=True))
    return shifted / jnp.sum(shifted, axis=1, keepdims=True)


def attend_kernel(
    tokens, w_query, w_key, w_value, gain, segment, bucket, table,
    normed_out, query_out, key_out, value_out, probs_out, mixed_out,
    band,
):
    length = tokens.shape[0]
    width = 2 * length
    heads = query_out.shape[1] // HDIM
    marks = bucket_marks(bucket, table.shape[1])
    table_rows = jnp.broadcast_to(table[...][:, None, :], (heads, 128, table.shape[1]))
    bases = []
    for h in range(heads):
        offsets = jnp.sum(
            jnp.where(marks, table_rows[h].T[:, 0:1], 0.0), axis=0, keepdims=True
        )
        bases.append(
            jnp.concatenate(
                [offsets] + [pltpu.roll(offsets, r, 1) for r in range(1, 8)], axis=0
            )
        )
    seg_row = segment[...].reshape(1, length)
    seg_col = as_column(seg_row)
    rows = tokens[...].astype(F32)
    normed = (rows * row_scale(rows) * gain[...].reshape(1, rows.shape[1])).astype(BF16)
    normed_out[...] = normed
    query = dot_nt(normed, w_query[...]).astype(BF16)
    key = dot_nt(normed, w_key[...]).astype(BF16)
    query_out[...] = query
    key_out[...] = key
    value_out[...] = dot_nt(normed, w_value[...]).astype(BF16)
    value_turned = dot_nt(w_value[...], normed).astype(BF16)
    for h in range(heads):
        cols = slice(h * HDIM, (h + 1) * HDIM)
        for b in range(length // 8):
            turned = pltpu.roll(bases[h], (length + 1 + 8 * b) % width, 1)
            band[8 * b : 8 * b + 8, :] = turned[:, :length]
        for c in range(0, length, CHUNK):
            span = slice(c, c + CHUNK)
            scores = dot_nt(query[span, cols], key[:, cols]) * SCORE_SCALE + band[span, :]
            scores = jnp.where(seg_col[span, :] == seg_row, scores, MASKED_SCORE)
            probs = softmax_rows(scores)
            probs_out[h, span, :] = probs
            mixed_out[cols, span] = dot_nt(value_turned[cols, :], probs.astype(BF16)).astype(BF16)


def dispatch(code, rows, outs, transposed=False):
    share = outs[0].shape[0]
    for k, out in enumerate(outs):
        ids = lax.broadcasted_iota(jnp.int32, (share, code.shape[1]), 0) + k * share
        marks = jnp.where(ids == code[...], 1.0, 0.0).astype(BF16)
        product = dot_nt if transposed else dot_nn
        out[...] = product(marks, rows).astype(BF16)


def slot_codes(meta, route, slot, size):
    count = route.shape[0]
    return ((route[...] ^ meta[1]) * size + slot[...]).reshape(1, count)


def first_kernel(
    meta, route, slot, cotangent, w_attn_out, w_router, gain, packed_out, *outs
):
    cap = outs[0].shape[1]
    count = len(outs) * cap
    code = slot_codes(meta, route, slot, cap)
    ids = lax.broadcasted_iota(jnp.int32, (count, code.shape[1]), 0)
    marks = jnp.where(ids == code, 1.0, 0.0).astype(BF16)
    placed = dot_nt(cotangent[...], marks).astype(BF16)
    for k, out in enumerate(outs):
        out[...] = placed[:, k * cap : (k + 1) * cap]
    rows, feats = w_attn_out.shape
    experts = w_router.shape[0]
    packed_out[:rows, :] = w_attn_out[...]
    length = cotangent.shape[1]
    top = packed_out.shape[0] - rows
    packed_out[top:, :length] = cotangent[...]
    packed_out[top:, length:] = jnp.zeros((rows, feats - length), BF16)
    line = gain[...].reshape(1, rows)
    high = line.astype(BF16)
    rest = line - high.astype(F32)
    mid = rest.astype(BF16)
    low = (rest - mid.astype(F32)).astype(BF16)
    pad = top - rows - experts - 3
    extra = [w_router[...].astype(F32)] + [p.astype(F32) for p in (high, mid, low)]
    extra = jnp.concatenate(extra + [jnp.zeros((pad, rows), F32)], axis=0)
    wide = jnp.concatenate([extra, jnp.zeros((extra.shape[0], feats - rows), F32)], axis=1)
    packed_out[rows:top, :] = wide.astype(BF16)


def dispatch(code, rows, outs):
    share = outs[0].shape[0]
    for k, out in enumerate(outs):
        ids = lax.broadcasted_iota(jnp.int32, (share, code.shape[1]), 0) + k * share
        marks = jnp.where(ids == code, 1.0, 0.0).astype(BF16)
        out[...] = dot_nn(marks, rows).astype(BF16)


def residual_kernel(
    meta, route, slot, m0, m1, m2, m3, w0, w1, w2, w3, tokens,
    residual_out, gate_out, probs_out, params_out, turned_out, *rest,
):
    outs, place, cot_place = rest[:-2], rest[-2], rest[-1]
    share = outs[0].shape[0]
    experts = probs_out.shape[1]
    cols = m0.shape[0]
    for j, w in enumerate((w0, w1, w2, w3)):
        place[meta[0] ^ j] = w[cols : w.shape[0] - cols, :cols].astype(F32)
        cot_place[meta[0] ^ j] = w[w.shape[0] - cols :, : tokens.shape[0]]
    for r in range(4):
        turned_out[r * cols : (r + 1) * cols, :] = cot_place[r]
    params = jnp.concatenate([place[r] for r in range(4)], axis=1)
    router = params[:experts]
    gain = params[experts : experts + 1]
    for i in (1, 2):
        gain = gain + params[experts + i : experts + i + 1]
    params_out[...] = jnp.concatenate([router, jnp.broadcast_to(gain, (8, gain.shape[1]))], axis=0)
    residual = tokens[...].astype(F32)
    for m, w in ((m0, w0), (m1, w1), (m2, w2), (m3, w3)):
        residual = residual + dot_tn(m[...], w[:cols, :])
    residual_out[...] = residual
    normed = residual * row_scale(residual) * gain
    part = slot[...] - meta[0] * share
    code = jnp.where(
        (part >= 0) & (part < share), (route[...] ^ meta[1]) * share + part, -1
    ).reshape(1, part.shape[0])
    dispatch(code, normed.astype(BF16), outs)
    probs = softmax_rows(dot_nt(normed, router, PRECISE))
    probs_out[...] = probs
    lanes = lax.broadcasted_iota(jnp.int32, probs.shape, 1)
    where = as_column(route[...].reshape(1, part.shape[0]))
    gate_out[...] = jnp.sum(jnp.where(lanes == where, probs, 0.0), axis=1, keepdims=True)


def assemble_kernel(*refs, count):
    out = refs[-1]
    size = refs[0].shape[0]
    for i, block in enumerate(refs[:count]):
        out[i * size : (i + 1) * size, :] = block[...]


def expert_kernel(
    meta, x0, x1, x2, x3, c0, c1, c2, c3, w_in, w_out, router,
    rows_out, act_out, cots_out, d_hidden_out, keep_out, send_out,
    x_all, c_all, part_all, *, first, direct,
):
    rank, expert = meta[0], meta[1]
    ranks = 4
    total = rows_out.shape[0]
    feats = rows_out.shape[1]
    cols = feats // ranks
    if direct:
        sources, _, share, _ = x_all.shape
        cap = ranks * share
        for j, (x, c) in enumerate(((x0, c0), (x1, c1), (x2, c2), (x3, c3))):
            for s in range(sources):
                x_all[s, rank ^ j] = x[s * share : (s + 1) * share, :]
                at = (first + s) * cols
                c_all[rank ^ j, :, s * cap : (s + 1) * cap] = c[at : at + cols, :]
        step = 256 // cap
    for i in range(total // 256):
        span = slice(i * 256, (i + 1) * 256)
        if direct:
            rows = x_all[i * step : (i + 1) * step].reshape(256, feats)
            turned = jnp.concatenate([c_all[r, :, span] for r in range(ranks)], axis=0)
            cots = turned.astype(F32).T.astype(BF16)
        else:
            rows = x0[span, :]
            cots = c0[span, :]
        rows_out[span, :] = rows
        probs = softmax_rows(dot_nt(rows, router[...].astype(BF16)))
        lanes = lax.broadcasted_iota(jnp.int32, probs.shape, 1)
        gate = jnp.sum(jnp.where(lanes == expert, probs, 0.0), axis=1, keepdims=True)
        cots_out[span, :] = (gate * cots.astype(F32)).astype(BF16)
        hidden = dot_nn(rows, w_in[...])
        pull = dot_nt(cots, w_out[...])
        bent = jnp.tanh(GELU_C * (hidden + GELU_A * hidden * hidden * hidden))
        act = (0.5 * hidden * (1.0 + bent)).astype(BF16)
        act_out[span, :] = act
        slope = 0.5 * (1.0 + bent) + 0.5 * hidden * (1.0 - bent * bent) * (
            GELU_C * (1.0 + 3.0 * GELU_A * hidden * hidden)
        )
        d_hidden = (gate * pull * slope).astype(BF16)
        d_hidden_out[span, :] = d_hidden
        d_gate = jnp.sum(pull * act.astype(F32), axis=1, keepdims=True)
        d_part = dot_nt(w_in[...], d_hidden).astype(BF16)
        tail = jnp.broadcast_to(d_gate, (256, 128)).T[: part_all.shape[1] - cols].astype(BF16)
        for r in range(ranks):
            j = rank ^ r
            place = (j % 2) * 2 + j // 2
            part_all[place, :cols, span] = d_part[r * cols : (r + 1) * cols, :]
            part_all[place, cols:, span] = tail
    keep_out[...] = part_all[0:2]
    send_out[...] = part_all[2:4]


def expert_out_kernel(meta, w_out, *refs, groups):
    acts, (keep_out, send_out, part_all) = refs[:groups], refs[-3:]
    rank = meta[0]
    ranks = 4
    cols = part_all.shape[1]
    at = 0
    for act in acts:
        for i in range(0, act.shape[0], 256):
            part = dot_nn(act[i : i + 256, :], w_out[...]).T.astype(BF16)
            for r in range(ranks):
                j = rank ^ r
                part_all[(j % 2) * 2 + j // 2, :, at : at + 256] = part[r * cols : (r + 1) * cols]
            at += 256
    keep_out[...] = part_all[0:2]
    send_out[...] = part_all[2:4]


def slot_marks(meta, route, slot, cap, count):
    code = slot_codes(meta, route, slot, cap)
    ids = lax.broadcasted_iota(jnp.int32, (code.shape[1], count), 1)
    return jnp.where(ids == as_column(code), 1.0, 0.0).astype(BF16)


def fence_kernel(*refs):
    del refs


def side_by_side(blocks, came):
    size = blocks[0].shape[1]
    for k, block in enumerate(blocks):
        came[:, k * size : (k + 1) * size] = block[...]
    return came[...]


def combine_kernel(meta, route, slot, *rest, cap):
    *blocks, _, out, came = rest
    marks = slot_marks(meta, route, slot, cap, came.shape[1])
    out[...] = dot_nt(side_by_side(blocks, came), marks).astype(BF16)


def block_out_kernel(meta, route, slot, residual, gate, *rest, cap):
    *blocks, block_out, came, place = rest
    rank = meta[0]
    cols = block_out.shape[1]
    marks = slot_marks(meta, route, slot, cap, came.shape[1])
    returned = dot_nt(marks, side_by_side(blocks, came))
    for r in range(4):
        place[r] = residual[:, r * cols : (r + 1) * cols]
    block_out[...] = (place[rank] + gate[...] * returned).astype(BF16)


def residual_back_kernel(
    meta, r0, r1, r2, r3, residual, gate, probs, route, params, cotangent, mixed, w_attn_out,
    attn_probs, normed_one, _, d_attn_cols_out, d_mixed_out, d_value_out, router_grad_out,
    gain_grad_out, *rest,
):
    attn_grad_out, value_grad_out, place, place_f32 = rest
    rank, expert = meta[0], meta[1]
    experts = probs.shape[1]
    feats = residual.shape[1]
    cols = feats // 4
    length = residual.shape[0]
    router = params[:experts, :]
    gain = params[experts : experts + 1, :]
    for j, r in enumerate((r0, r1, r2, r3)):
        place[rank ^ j] = r[:cols, :]
    d_gate = as_column(r0[cols : cols + 1, :].astype(F32))
    d_routed = jnp.concatenate([place[r] for r in range(4)], axis=0).astype(F32).T
    res = residual[...]
    scale = row_scale(res)
    lanes = lax.broadcasted_iota(jnp.int32, probs.shape, 1)
    onehot = jnp.where(lanes == as_column(route[...].reshape(1, length)), 1.0, 0.0)
    d_logits = d_gate * probs[...] * (onehot - gate[...])
    d_normed = d_routed + dot_nn(d_logits, router, PRECISE)
    normed = res * scale * gain
    router_grad = dot_tn(d_logits, normed, PRECISE)
    gain_grad = jnp.sum(d_normed * res * scale, axis=0, keepdims=True)
    cross = jnp.sum(gain * res * d_normed, axis=1, keepdims=True)
    d_residual = (
        cotangent[...].astype(F32).T
        + scale * gain * d_normed
        - res * (scale * scale * scale * cross * (1.0 / feats))
    )
    for r in range(4):
        own = slice(r * cols, (r + 1) * cols)
        place_f32[r] = d_residual[:, own]

        @pl.when(rank == r)
        def _():
            router_grad_out[...] = router_grad[:, own]
            gain_grad_out[...] = gain_grad[:, own]

    d_attn_cols_out[...] = place_f32[rank]
    d_attn = d_residual.astype(BF16)
    attn_grad_out[...] = dot_nn(mixed[...], d_attn).astype(BF16)
    d_mixed = dot_nt(d_attn, w_attn_out[...]).astype(BF16)
    d_mixed_out[...] = d_mixed
    for h in range(cols // HDIM):
        own = slice(h * HDIM, (h + 1) * HDIM)
        total = jnp.zeros((length, HDIM), F32)
        for c in range(0, length, CHUNK):
            span = slice(c, c + CHUNK)
            total = total + dot_tn(attn_probs[h, span, :].astype(BF16), d_mixed[span, own])
        d_value_out[:, own] = total.astype(BF16)
    value_grad_out[...] = dot_tn(d_value_out[...], normed_one[...]).astype(BF16)


def attend_back_kernel(
    query, key, value, probs, d_mixed, bucket, d_query, d_key, table_out, *, buckets
):
    length = query.shape[0]
    width = 2 * length
    heads = query.shape[1] // HDIM
    marks = bucket_marks(bucket, buckets)
    zeros = jnp.zeros((8, width - length), F32)
    table_out[...] = jnp.zeros(table_out.shape, F32)
    for h in range(heads):
        own = slice(h * HDIM, (h + 1) * HDIM)
        dk = jnp.zeros((length, HDIM), F32)
        diagonals = jnp.zeros((8, width), F32)
        for c in range(0, length, CHUNK):
            span = slice(c, c + CHUNK)
            weights = probs[h, span, :]
            d_probs = dot_nt(d_mixed[span, own], value[:, own])
            inner = jnp.sum(d_probs * weights, axis=1, keepdims=True)
            d_scores = weights * (d_probs - inner)
            for b in range(CHUNK // 8):
                piece = jnp.concatenate([d_scores[8 * b : 8 * b + 8, :], zeros], axis=1)
                diagonals = diagonals + pltpu.roll(piece, (length - 1 - c - 8 * b) % width, 1)
            low = d_scores.astype(BF16)
            d_query[span, own] = (dot_nn(low, key[:, own]) * SCORE_SCALE).astype(BF16)
            dk = dk + dot_tn(low, query[span, own])
        d_key[:, own] = (dk * SCORE_SCALE).astype(BF16)
        line = diagonals[0:1]
        for r in range(1, 8):
            line = line + pltpu.roll(diagonals[r : r + 1], width - r, 1)
        table_col = jnp.sum(jnp.where(marks, line, 0.0), axis=1, keepdims=True)
        table_out[h : h + 1, :buckets] = jnp.broadcast_to(table_col, (buckets, 128)).T[0:1, :]


def put_split(out, at, row, value):
    high = value.astype(BF16).astype(F32)
    out[row : row + 1, at : at + value.shape[1]] = high
    out[row + 8 : row + 9, at : at + value.shape[1]] = value - high


def query_back_kernel(
    meta, tokens, gain, normed, d_query, d_key, d_value, w_query, w_key, w_value, gain2_grad,
    table_grad, router_grad, _, *rest, chunked, heads, buckets,
):
    keep_in, send_in, gain1_out, first_out, second_out, place, chunk_place, pack = rest
    rank, expert = meta[0], meta[1]
    length, feats = tokens.shape
    cols = feats // 4
    normed_rows = normed[...]
    query_grad = dot_tn(d_query[...], normed_rows).astype(BF16)
    key_grad = dot_tn(d_key[...], normed_rows).astype(BF16)
    d_normed = (
        dot_nn(d_query[...], w_query[...])
        + dot_nn(d_key[...], w_key[...])
        + dot_nn(d_value[...], w_value[...])
    )
    rows = tokens[...].astype(F32)
    product = d_normed * rows
    gain1_grad = jnp.sum(product * row_scale(rows), axis=0, keepdims=True)
    gain1_out[...] = jnp.broadcast_to(gain1_grad, gain1_out.shape)
    if chunked:
        pack[...] = jnp.zeros(pack.shape, F32)
        put_split(pack, 0, 0, gain1_grad)
        put_split(pack, 0, 1, gain2_grad[...])
        for h in range(heads):
            put_split(pack, 256 * h, 2, table_grad[h : h + 1, :])
        for e in range(router_grad.shape[0]):
            put_split(pack, 256 * (e % 3), 3 + e // 3, router_grad[e : e + 1, :])
        small = pack[...].astype(BF16)
        both = jnp.concatenate([query_grad, key_grad], axis=0)
        count = len(chunked)
        size = both.shape[0] // count
        for c in range(count):
            chunk_place[c ^ expert] = both[c * size : (c + 1) * size, :]
        for i, k in enumerate(chunked):
            out = first_out if i < count // 2 else second_out
            at = (i % (count // 2)) * size
            out[at : at + size, :] = chunk_place[k]
        for out in (first_out, second_out):
            out[out.shape[0] - 16 :, :] = small
    else:
        first_out[...] = query_grad
        second_out[...] = key_grad
    cross = jnp.sum(product * gain[...].reshape(1, feats), axis=1, keepdims=True)
    high = cross.astype(BF16).astype(F32)
    low = cross - high
    lanes = lax.broadcasted_iota(jnp.int32, (length, place.shape[2] - cols), 1)
    extra = jnp.where(lanes == 0, high, jnp.where(lanes == 1, low, 0.0)).astype(BF16)
    for r in range(4):
        j = rank ^ r
        own = d_normed[:, r * cols : (r + 1) * cols].astype(BF16)
        place[(j % 2) * 2 + j // 2] = jnp.concatenate([own, extra], axis=1)
    keep_in[...] = place[0:2]
    send_in[...] = place[2:4]


def input_kernel(
    meta, tokens, gain, d_attn_cols, first, second, *rest
):
    *_, out, place, gain_place = rest
    rank = meta[0]
    feats = tokens.shape[1]
    cols = feats // 4
    rows = tokens[...].astype(F32)
    scale = row_scale(rows)
    both = first[...].astype(F32) + second[...].astype(F32)
    cross = both[:, cols : cols + 1] + both[:, cols + 1 : cols + 2]
    gain_row = gain[...].reshape(1, feats)
    for r in range(4):
        place[r] = rows[:, r * cols : (r + 1) * cols]
        gain_place[r] = gain_row[:, r * cols : (r + 1) * cols]
    own = both[:, :cols]
    own_rows = place[rank]
    out[...] = (
        d_attn_cols[...]
        + scale * gain_place[rank] * own
        - own_rows * (scale * scale * scale * cross * (1.0 / feats))
    )


def add_small(a, b):
    at = a.shape[0] - 16
    total = (
        a[at : at + 8, :].astype(F32)
        + b[at : at + 8, :].astype(F32)
        + a[at + 8 :, :].astype(F32)
        + b[at + 8 :, :].astype(F32)
    )
    high = total.astype(BF16).astype(F32)
    return total, jnp.concatenate([high, total - high], axis=0).astype(BF16)


def sum_kernel(keep, got, keep_out, send_out):
    half = (keep.shape[0] - 16) // 2
    total = (keep[: 2 * half, :].astype(F32) + got[: 2 * half, :].astype(F32)).astype(BF16)
    _, small = add_small(keep, got)
    keep_out[:half, :] = total[:half]
    send_out[:half, :] = total[half:]
    keep_out[half:, :] = small
    send_out[half:, :] = small


def last_sum_kernel(keep, got, mine_out, small_out, gain1_out):
    size = mine_out.shape[0]
    mine_out[...] = (keep[:size, :].astype(F32) + got[:size, :].astype(F32)).astype(BF16)
    total, _ = add_small(keep, got)
    small_out[...] = total
    gain1_out[...] = jnp.broadcast_to(total[0:1], gain1_out.shape)


def finish_kernel(
    meta, mine, second, other, small, attn, value, *rest, order, heads
):
    attn_out, value_out, first_out, second_out, gain2_out, table_out, router_out, place = rest[-8:]
    attn_out[...] = attn[...].astype(F32)
    value_out[...] = value[...].astype(F32)
    expert = meta[1]
    count = len(order)
    size = mine.shape[0] // 2
    quarter = count // 4
    for i in range(count):
        block, at = (
            (mine, i)
            if i < quarter
            else (second, i - quarter) if i < 2 * quarter else (other, i - 2 * quarter)
        )
        place[order[i]] = block[at * size : (at + 1) * size, :]
    rows = first_out.shape[0]
    for c in range(count):
        chunk = place[c ^ expert].astype(F32)
        start = c * size
        if start < rows:
            first_out[start : start + size, :] = chunk
        else:
            second_out[start - rows : start - rows + size, :] = chunk
    cols = gain2_out.shape[1]
    gain2_out[...] = small[1:2, :cols]
    for h in range(heads):
        table_out[h : h + 1, :] = small[2:3, 256 * h : 256 * h + table_out.shape[1]]
    for e in range(router_out.shape[0]):
        at = 256 * (e % 3)
        router_out[e : e + 1, :] = small[3 + e // 3 : 4 + e // 3, at : at + cols]


def fetching(kernel, smem, fetch):
    def run(*refs):
        scalars, far = refs[:smem], refs[smem : smem + fetch]
        rest, near, sems = refs[smem + fetch : -fetch - 1], refs[-fetch - 1 : -1], refs[-1]
        copies = [
            pltpu.make_async_copy(a, b, sems.at[i]) for i, (a, b) in enumerate(zip(far, near))
        ]
        for copy in copies:
            copy.start()
        for copy in copies:
            copy.wait()
        kernel(*scalars, *near, *rest)

    return run


def call(kernel, outs, scratch, *operands, weight=1.0, smem=1, fetch=0, after=()):
    specs = []
    for i in range(len(operands)):
        if i < smem:
            specs.append(pl.BlockSpec(memory_space=pltpu.SMEM))
        elif i < smem + fetch:
            specs.append(pl.BlockSpec(memory_space=pltpu.HBM))
        else:
            specs.append(pl.BlockSpec(memory_space=pltpu.VMEM))
    specs += [pl.BlockSpec(memory_space=pl.ANY)] * len(after)
    scratch_shapes = [pltpu.VMEM(shape, kind) for shape, kind in scratch]
    if fetch:
        kernel = fetching(kernel, smem, fetch)
        scratch_shapes += [pltpu.VMEM(a.shape, a.dtype) for a in operands[smem : smem + fetch]]
        scratch_shapes.append(pltpu.SemaphoreType.DMA((fetch,)))
    return pl.pallas_call(
        kernel,
        out_shape=[jax.ShapeDtypeStruct(shape, kind) for shape, kind in outs],
        in_specs=specs,
        out_specs=[pl.BlockSpec(memory_space=pltpu.VMEM)] * len(outs),
        scratch_shapes=scratch_shapes,
        compiler_params=pltpu.CompilerParams(vmem_limit_bytes=28 * 1024 * 1024),
        cost_estimate=pl.CostEstimate(
            flops=int(weight * 1.1e9), bytes_accessed=1 << 16, transcendentals=0
        ),
    )(*operands, *after)


def swap(array, axis, bit):
    size = lax.axis_size(axis)
    return lax.ppermute(array, axis, [(i, i ^ bit) for i in range(size)])


def add_low(a, b):
    return (a.astype(F32) + b.astype(F32)).astype(BF16)


def gather_four(array):
    across = swap(array, "tensor", 2)
    beside = swap(array, "tensor", 1)
    return [array, beside, across, swap(across, "tensor", 1)]


def reduce_four(keep, send):
    got = swap(send, "tensor", 1)
    far = add_low(keep[1], got[1])
    return add_low(keep[0], got[0]), swap(far, "tensor", 2), far


def exchange(blocks):
    if len(blocks) > 8:
        return hyper_exchange(blocks)[0]
    return [blocks[0]] + [swap(b, "expert", k) for k, b in enumerate(blocks) if k]


def hyper_exchange(blocks, after=()):
    count = len(blocks)
    held = {k: [b] for k, b in enumerate(blocks)}
    steps = []
    bit = 1
    while bit < count:
        away = [k for k in sorted(held) if k & bit]
        sent = jnp.concatenate([b for k in away for b in held[k]], axis=0)
        got = swap(sent, "expert", bit)
        if bit == 1 and after:
            (got,) = fence([got], after)
        steps.append(got)
        size = blocks[0].shape[0]
        at = 0
        fresh = {}
        for k in away:
            pieces = [got[at + i * size : at + (i + 1) * size] for i in range(len(held[k]))]
            at += len(held[k]) * size
            fresh[k ^ bit] = held[k ^ bit] + pieces
        held = fresh
        bit *= 2
    return held[0], steps


ORDER = (0, 4, 2, 6, 1, 5, 3, 7)


def halve(keep, send):
    feats = keep.shape[1]
    for bit in (1, 2):
        rows = (keep.shape[0] - 16) // 2 + 16
        keep, send = call(
            sum_kernel, [((rows, feats), BF16)] * 2, [], keep, swap(send, "expert", bit), smem=0
        )
    return call(
        last_sum_kernel,
        [((keep.shape[0] - 16, feats), BF16), ((8, feats), F32), ((8, feats), F32)],
        [],
        keep, swap(send, "expert", 4), smem=0,
    )


def fence(arrays, after):
    count = len(arrays)
    return pl.pallas_call(
        fence_kernel,
        out_shape=[jax.ShapeDtypeStruct(a.shape, a.dtype) for a in arrays],
        in_specs=[pl.BlockSpec(memory_space=pl.ANY)] * (count + len(after)),
        out_specs=[pl.BlockSpec(memory_space=pl.ANY)] * count,
        input_output_aliases={i: i for i in range(count)},
    )(*arrays, *after)


def on_device(
    tokens, cotangent, norm1_gain, w_query, w_key, w_value, w_attn_out, bias_table, norm2_gain,
    w_router, expert_in, expert_out, route, slot, segment, rel_bucket,
):
    length, feats = tokens.shape
    cols = cotangent.shape[1]
    heads = cols // HDIM
    experts = lax.axis_size("expert")
    cap = 2 * length // experts
    share = cap // 4
    rank = lax.axis_index("tensor").astype(jnp.int32)
    expert = lax.axis_index("expert").astype(jnp.int32)
    meta = jnp.stack([rank, expert])
    total = experts * cap
    direct = share % 16 == 0
    buckets = bias_table.shape[0]
    chunked = ORDER if experts == len(ORDER) else None

    w_query_t, w_key_t, w_value_t = w_query.T, w_key.T, w_value.T
    packed_rows = 2 * cols + -(-(experts + 3) // 16) * 16
    packed, *cot_blocks = call(
        first_kernel,
        [((packed_rows, feats), BF16)] + [((cols, cap), BF16)] * experts,
        [],
        meta, route, slot, cotangent.T, w_attn_out, w_router.T, norm2_gain,
        weight=2.0, fetch=6,
    )
    packed_parts = gather_four(packed)
    bucket = jnp.concatenate([rel_bucket, jnp.full((1,), -1, jnp.int32)])
    normed, query, key, value, probs, mixed = call(
        attend_kernel,
        [((length, feats), BF16)]
        + [((length, cols), BF16)] * 3
        + [((heads, length, length), F32), ((cols, length), BF16)],
        [((length, length), F32)],
        tokens, w_query.T, w_key.T, w_value.T, norm1_gain, segment, bucket, bias_table.T,
        weight=7.0, smem=0, fetch=8,
    )

    mixed_parts = gather_four(mixed)
    cot_arrived, _ = hyper_exchange(cot_blocks, (mixed, packed_parts[1], packed_parts[2]))
    residual, gate, router_probs, params, cot_turned, *row_blocks = call(
        residual_kernel,
        [
            ((length, feats), F32),
            ((length, 1), F32),
            ((length, experts), F32),
            ((experts + 8, feats), F32),
            ((feats, length), BF16),
        ]
        + [((share, feats), BF16)] * experts,
        [((4, packed_rows - 2 * cols, cols), F32), ((4, cols, length), BF16)],
        meta, route, slot, *mixed_parts, *packed_parts, tokens,
        weight=5.8,
    )
    (cot_own,) = fence([jnp.concatenate(cot_arrived, axis=0)], (residual,))
    cot_rows = gather_four(cot_own)
    arrived = exchange(row_blocks)
    groups = GROUPS if direct else 1
    group_size = experts // groups
    row_groups = []
    for g in range(groups):
        blocks = arrived[g * group_size : (g + 1) * group_size]
        if direct:
            (packed,) = call(
                functools.partial(assemble_kernel, count=group_size),
                [((group_size * share, feats), BF16)],
                [],
                *blocks,
                weight=1.0, smem=0, after=(cot_rows[2],),
            )
        else:
            packed = jnp.concatenate(blocks, axis=0)
        row_groups.append(gather_four(packed))

    if not direct:
        def assemble(parts, shape, turn):
            stacked = jnp.stack(parts).reshape(4, experts, *shape)
            stacked = stacked[rank ^ jnp.arange(4, dtype=jnp.int32)]
            return [jnp.transpose(stacked, turn).reshape(total, feats)]

        one = jnp.zeros((16, 128), BF16)
        row_groups = [assemble(row_groups[0], (share, feats), (1, 0, 2, 3)) + [one] * 3]
        cot_rows = assemble(cot_rows, (cols, cap), (1, 3, 0, 2)) + [one] * 3
    w_in, w_out = expert_in[0], expert_out[0]
    hidden_count = w_in.shape[1]
    part_rows = cols + 16
    count = total // groups
    x_shape = (group_size, 4, share, feats) if direct else (1, 1, 16, 128)
    c_shape = (4, cols, count) if direct else (1, 16, 128)
    acts, returning, kept = [], [], []
    for g in range(groups):
        rows_all, act, cots, d_hidden, keep, send = call(
            functools.partial(expert_kernel, first=g * group_size, direct=direct),
            [((count, feats), BF16), ((count, hidden_count), BF16), ((count, feats), BF16),
             ((count, hidden_count), BF16), ((2, part_rows, count), BF16),
             ((2, part_rows, count), BF16)],
            [(x_shape, BF16), (c_shape, BF16), ((4, part_rows, count), BF16)],
            meta, *row_groups[g], *cot_rows, w_in, w_out, params[:experts],
            weight=10.0,
        )
        near, far, _ = reduce_four(keep, send)
        whole = add_low(near, far)
        returning += [whole[:, k * cap : (k + 1) * cap] for k in range(group_size)]
        acts.append(act)
        kept += [act, cots, rows_all, d_hidden]

    def unite(blocks):
        return blocks if cap % 128 == 0 else [jnp.concatenate(blocks, axis=1)]

    keep_fwd, send_fwd = call(
        functools.partial(expert_out_kernel, groups=groups),
        [((2, cols, total), BF16)] * 2,
        [((4, cols, total), BF16)],
        meta, w_out, *acts,
        weight=2.9, after=(whole,),
    )
    (d_routed,) = call(
        functools.partial(combine_kernel, cap=cap),
        [((part_rows, length), BF16)],
        [((part_rows, total), BF16)],
        meta, route, slot, *unite(exchange(returning)), after=(keep_fwd,),
        weight=1.0,
    )
    routed_parts = gather_four(d_routed)

    near_fwd, far_fwd, met_fwd = reduce_four(keep_fwd, send_fwd)
    whole_fwd = add_low(near_fwd, far_fwd)
    fwd_arrived, fwd_steps = hyper_exchange(
        [whole_fwd[:, k * cap : (k + 1) * cap] for k in range(experts)]
    )
    came_fwd = unite(fwd_arrived)
    (block_out,) = call(
        functools.partial(block_out_kernel, cap=cap),
        [((length, cols), BF16)],
        [((cols, total), BF16), ((4, length, cols), F32)],
        meta, route, slot, residual, gate, *came_fwd,
        weight=1.2,
    )

    d_attn_cols, d_mixed, d_value, router_grad, gain2_grad, *first_grads = call(
        residual_back_kernel,
        [((length, cols), F32), ((length, cols), BF16), ((length, cols), BF16),
         ((experts, cols), F32), ((1, cols), F32)] + [((cols, feats), BF16)] * 2,
        [((4, cols, length), BF16), ((4, length, cols), F32)],
        meta, *routed_parts, residual, gate, router_probs, route, params, cot_turned, mixed,
        w_attn_out, probs, normed, after=(met_fwd,),
        weight=8.0,
    )
    d_query, d_key, table_grad = call(
        functools.partial(attend_back_kernel, buckets=buckets),
        [((length, cols), BF16)] * 2 + [((8, 128), F32)],
        [],
        query, key, value, probs, d_mixed, bucket, smem=0,
        weight=7.0,
    )
    wide = -(-(cols + 2) // 128) * 128
    if chunked:
        size = 2 * cols // experts
        grad_outs = [((experts // 2 * size + 16, feats), BF16)] * 2
        chunk_scratch = ((experts, size, feats), BF16)
    else:
        grad_outs = [((cols, feats), BF16)] * 2
        chunk_scratch = ((16, 128), BF16)
    keep_in, send_in, gain1_grad, *second_grads = call(
        functools.partial(query_back_kernel, chunked=chunked, heads=heads, buckets=buckets),
        [((2, length, wide), BF16)] * 2 + [((8, feats), F32)] + grad_outs,
        [((4, length, wide), BF16), chunk_scratch, ((16, feats), F32)],
        meta, tokens, norm1_gain, normed, d_query, d_key, d_value, w_query_t, w_key_t,
        w_value_t, gain2_grad, table_grad, router_grad, after=(whole_fwd,),
        weight=4.0,
    )
    first_grads = lax.psum(tuple(first_grads), "expert")
    near_in, far_in, met_in = reduce_four(keep_in, send_in)
    (input_grad,) = call(
        input_kernel,
        [((length, cols), F32)],
        [((4, length, cols), F32), ((4, 1, cols), F32)],
        meta, tokens, norm1_gain, d_attn_cols, near_in, far_in,
        weight=1.0,
    )

    kept = fence(kept, (met_in,))
    expert_out_grad = sum(dot_tn(kept[4 * g], kept[4 * g + 1]) for g in range(groups))
    expert_in_grad = sum(dot_tn(kept[4 * g + 2], kept[4 * g + 3]) for g in range(groups))
    if chunked:
        mine, small, gain1_grad = halve(*second_grads)
        held = jnp.concatenate([mine, swap(mine, "expert", 4)], axis=0)
        beside = swap(held, "expert", 2)
        other = swap(jnp.concatenate([held, beside], axis=0), "expert", 1)
        for bit in (1, 2):
            gain1_grad = gain1_grad + swap(gain1_grad, "tensor", bit)
        attn_grad, value_grad, query_grad, key_grad, gain2_grad, table_grad, router_grad = call(
            functools.partial(finish_kernel, order=ORDER, heads=heads),
            [((cols, feats), F32)] * 4
            + [((1, cols), F32), ((heads, buckets), F32), ((experts, cols), F32)],
            [chunk_scratch],
            meta, held, beside, other, small, *first_grads,
            weight=1.6, after=(input_grad, block_out, gain1_grad),
        )
    else:
        query_grad, key_grad, gain2_grad, table_grad, router_grad = lax.psum(
            (*second_grads, gain2_grad, table_grad[:heads, :buckets], router_grad), "expert"
        )
        gain1_grad = lax.psum(gain1_grad, ("expert", "tensor"))
        attn_grad, value_grad = first_grads
    return (
        block_out,
        input_grad,
        gain1_grad[0],
        query_grad.astype(F32).T,
        key_grad.astype(F32).T,
        value_grad.astype(F32).T,
        attn_grad.astype(F32),
        table_grad.T,
        gain2_grad[0],
        router_grad.T,
        expert_in_grad[None],
        expert_out_grad[None],
    )


def solution(mesh):
    return jax.shard_map(
        on_device,
        mesh=mesh,
        in_specs=(
            P("expert", None),
            P("expert", "tensor"),
            P(),
            P(None, "tensor"),
            P(None, "tensor"),
            P(None, "tensor"),
            P("tensor", None),
            P(None, "tensor"),
            P("tensor"),
            P("tensor", None),
            P("expert", None, "tensor"),
            P("expert", "tensor", None),
            P("expert"),
            P("expert"),
            P("expert"),
            P(),
        ),
        out_specs=(
            P("expert", "tensor"),
            P("expert", "tensor"),
            P(),
            P(None, "tensor"),
            P(None, "tensor"),
            P(None, "tensor"),
            P("tensor", None),
            P(None, "tensor"),
            P("tensor"),
            P("tensor", None),
            P("expert", None, "tensor"),
            P("expert", "tensor", None),
        ),
        check_vma=False,
    )
```

profile of v0, /device:TPU:0, one launch (start us, length us, event | category | flops | bytes accessed | tf_op | source)
XLA Modules:
  0.0 255.1 jit_solution(7391300129290185588)
XLA Ops:
  7.3 1.0 copy-done.20
  8.3 0.9 copy-done.30
  12.0 1.5 shard_map.248
  13.5 3.0 %collective-permute-start.4 = (bf16[400,768]{1,0:T(8,128)(2,1)S(1)}, bf16[400,768]{1,0:T(8,128)(2,1)S(1)}, u32[]{:S(2)}, u32[]{:S(2)}) collective-permute-start(bf16[400,768]{1,0:T(8,128)(2,1)S(1)} %get-tuple-element.81.w0), channel_id=1, source_target_pairs={{0,2},{1,3},{2,0},{3,1},{4,6},{5,7},{6,4},{7,5},{8,10},{9,11},{10,... | collective-permute-start | bytes 1843208 | tf_op jit(solution)/shard_map/ppermute | solution.py:596
  16.6 1.6 collective-permute-start.13
  18.2 4.3 %shard_map.247 = (bf16[512,768]{1,0:T(8,128)(2,1)S(1)}, bf16[512,192]{1,0:T(8,128)(2,1)S(1)}, bf16[512,192]{1,0:T(8,128)(2,1)S(1)}, bf16[512,192]{1,0:T(8,128)(2...) custom-call(bf16[512,768]{1,0:T(8,128)(2,1)S(1)} %copy-done.17, bf16[192,768]{1,0:T(8,128)(2,1)S(1)} %bitcast.45, ...), custom_call_target="tpu_custom_call" | custom-call | flops 7699999744 | bytes 65536 | tf_op jit(solution)/shard_map/pallas_call | solution.py:581
  23.2 1.7 copy-done.50
  27.8 2.6 %collective-permute-done.4.w2.refs_3_ = bf16[400,768]{1,0:T(8,128)(2,1)S(1)} collective-permute-done((bf16[400,768]{1,0:T(8,128)(2,1)S(1)}, bf16[400,768]{1,0:T(8,128)(2,1)S(1)}, u32[]{:S(2)}, u32[]{:S(2)}) %collective-permute-start.4) | collective-permute-done | bytes 614432 | tf_op jit(solution)/shard_map/ppermute | solution.py:596
  31.4 1.0 fusion.13
  32.4 1.9 collective-permute-start.14
  34.3 1.5 collective-permute-start.1
  35.8 2.8 %collective-permute-done.14 = bf16[768,128]{1,0:T(8,128)(2,1)S(1)} collective-permute-done((bf16[768,128]{1,0:T(8,128)(2,1)S(1)}, bf16[768,128]{1,0:T(8,128)(2,1)S(1)}, u32[]{:S(2)}, u32[]{:S(2)}) %collective-permute-start.14) | collective-permute-done | bytes 196640 | tf_op jit(solution)/shard_map/ppermute | solution.py:596
  38.6 2.6 %collective-permute-start.15 = (bf16[768,128]{1,0:T(8,128)(2,1)S(1)}, bf16[768,128]{1,0:T(8,128)(2,1)S(1)}, u32[]{:S(2)}, u32[]{:S(2)}) collective-permute-start(bf16[768,128]{1,0:T(8,128)(2,1)S(1)} %pad_maximum_fusion.4), channel_id=1, source_target_pairs={{0,16},{4,20},{8,24},{12,28},{16,0},{20,4},{24,8},{28,12},{1,17},{... | collective-permute-start | bytes 589832 | tf_op jit(solution)/shard_map/ppermute | solution.py:596
  41.7 7.3 %collective-permute-done.15 = bf16[768,128]{1,0:T(8,128)(2,1)S(1)} collective-permute-done((bf16[768,128]{1,0:T(8,128)(2,1)S(1)}, bf16[768,128]{1,0:T(8,128)(2,1)S(1)}, u32[]{:S(2)}, u32[]{:S(2)}) %collective-permute-start.15) | collective-permute-done | bytes 196640 | tf_op jit(solution)/shard_map/ppermute | solution.py:596
  49.8 5.6 %shard_map.249 = (f32[512,768]{1,0:T(8,128)S(1)}, f32[512,1]{1,0:T(8,128)S(1)}, f32[512,8]{1,0:T(8,128)S(1)}, f32[16,768]{1,0:T(8,128)S(1)}, bf16[768,512]{1,0:T...) custom-call(s32[2]{0:T(128)S(1)} %pad_add_fusion.1.refs_0_.meta, ...), custom_call_target="tpu_custom_call" | custom-call | flops 6380000256 | bytes 65536 | tf_op jit(solution)/shard_map/pallas_call | solution.py:581
  55.4 1.1 copy-done
  57.2 1.1 collective-permute-start.16
  58.3 1.5 collective-permute-start.6
  60.5 1.3 collective-permute-start.8
  61.8 2.1 collective-permute-start.9
  63.9 1.8 collective-permute-start.10
  65.7 3.5 %collective-permute-start.11 = (bf16[32,768]{1,0:T(8,128)(2,1)S(1)}, bf16[32,768]{1,0:T(8,128)(2,1)S(1)}, u32[]{:S(2)}, u32[]{:S(2)}) collective-permute-start(bf16[32,768]{1,0:T(8,128)(2,1)S(1)} %get-tuple-element.90), channel_id=1, source_target_pairs={{0,24},{4,28},{8,16},{12,20},{16,8},{20,12},{24,0},{28,4},{1,25},{... | collective-permute-start | bytes 147464 | tf_op jit(solution)/shard_map/ppermute | solution.py:596
  70.6 1.8 collective-permute-done.11.refs_6_
  72.4 3.6 %collective-permute-done.12.refs_7_ = bf16[32,768]{1,0:T(8,128)(2,1)S(1)} collective-permute-done((bf16[32,768]{1,0:T(8,128)(2,1)S(1)}, bf16[32,768]{1,0:T(8,128)(2,1)S(1)}, u32[]{:S(2)}, u32[]{:S(2)}) %collective-permute-start.12) | collective-permute-done | bytes 49184 | tf_op jit(solution)/shard_map/ppermute | solution.py:596
  77.5 6.4 %collective-permute-done.18.x2 = bf16[256,768]{1,0:T(8,128)(2,1)S(1)} collective-permute-done((bf16[256,768]{1,0:T(8,128)(2,1)S(1)}, bf16[256,768]{1,0:T(8,128)(2,1)S(1)}, u32[]{:S(2)}, u32[]{:S(2)}) %collective-permute-start.18) | collective-permute-done | bytes 393248 | tf_op jit(solution)/shard_map/ppermute | solution.py:596
  83.9 1.7 collective-permute-done.19.x3
  85.6 7.3 %shard_map.253 = (bf16[1024,768]{1,0:T(8,128)(2,1)S(1)}, bf16[1024,768]{1,0:T(8,128)(2,1)S(1)}, bf16[1024,768]{1,0:T(8,128)(2,1)S(1)}, bf16[1024,768]{1,0:T(8,12...) custom-call(s32[2]{0:T(128)S(1)} %pad_add_fusion.1.refs_0_.meta, ...), custom_call_target="tpu_custom_call" | custom-call | flops 11000000512 | bytes 65536 | tf_op jit(solution)/shard_map/pallas_call | solution.py:581
  92.9 1.2 copy-done.3
  94.2 1.1 copy-done.6
  95.3 1.1 copy-done.8
  96.6 2.2 collective-permute-done.22
  99.5 11.4 %collective-permute-done.23 = bf16[208,1024]{1,0:T(8,128)(2,1)S(1)} collective-permute-done((bf16[208,1024]{1,0:T(8,128)(2,1)S(1)}, bf16[208,1024]{1,0:T(8,128)(2,1)S(1)}, u32[]{:S(2)}, u32[]{:S(2)}) %collective-permute-start.23) | collective-permute-done | bytes 426016 | tf_op jit(solution)/shard_map/ppermute | solution.py:596
  111.1 2.2 shard_map.254
  114.3 3.1 %collective-permute-start.34 = (bf16[208,128]{1,0:T(8,128)(2,1)S(1)}, bf16[208,128]{1,0:T(8,128)(2,1)S(1)}, u32[]{:S(2)}, u32[]{:S(2)}) collective-permute-start(bf16[208,128]{1,0:T(8,128)(2,1)S(1)} %get-tuple-element.165), channel_id=1, source_target_pairs={{0,24},{4,28},{8,16},{12,20},{16,8},{20,12},{24,0},{28,4},{1,25},{... | collective-permute-start | bytes 159752 | tf_op jit(solution)/shard_map/ppermute | solution.py:596
  117.4 3.8 %collective-permute-start.32 = (bf16[208,128]{1,0:T(8,128)(2,1)S(1)}, bf16[208,128]{1,0:T(8,128)(2,1)S(1)}, u32[]{:S(2)}, u32[]{:S(2)}) collective-permute-start(bf16[208,128]{1,0:T(8,128)(2,1)S(1)} %get-tuple-element.167), channel_id=1, source_target_pairs={{0,16},{4,20},{8,24},{12,28},{16,0},{20,4},{24,8},{28,12},{1,17},{... | collective-permute-start | bytes 159752 | tf_op jit(solution)/shard_map/ppermute | solution.py:596
  121.3 2.0 collective-permute-start.30
  123.3 2.0 collective-permute-done.33.rest_5_
  126.0 1.4 collective-permute-done.31.rest_3_
  127.4 1.9 collective-permute-done.29.rest_1_
  129.4 1.2 shard_map.256.r0
  131.2 5.3 %collective-permute-done.37.r2 = bf16[208,512]{1,0:T(8,128)(2,1)S(1)} collective-permute-done((bf16[208,512]{1,0:T(8,128)(2,1)S(1)}, bf16[208,512]{1,0:T(8,128)(2,1)S(1)}, u32[]{:S(2)}, u32[]{:S(2)}) %collective-permute-start.37) | collective-permute-done | bytes 213024 | tf_op jit(solution)/shard_map/ppermute | solution.py:596
  138.1 16.5 %shard_map.257 = (f32[512,192]{1,0:T(8,128)S(1)}, bf16[512,192]{1,0:T(8,128)(2,1)S(1)}, bf16[512,192]{1,0:T(8,128)(2,1)S(1)}, f32[8,192]{1,0:T(8,128)S(1)}, f32[...) custom-call(s32[2]{0:T(128)S(1)} %pad_add_fusion.1.refs_0_.meta, ...), custom_call_target="tpu_custom_call" | custom-call | flops 8800000000 | bytes 65536 | tf_op jit(solution)/shard_map/pallas_call | solution.py:581
  154.5 4.7 %shard_map.258 = (bf16[512,192]{1,0:T(8,128)(2,1)S(1)}, bf16[512,192]{1,0:T(8,128)(2,1)S(1)}, f32[8,128]{1,0:T(8,128)S(1)}) custom-call(bf16[512,192]{1,0:T(8,128)(2,1)S(1)} %copy-done.57, bf16[512,192]{1,0:T(8,128)(2,1)S(1)} %copy-done.59, bf16[512,192]{1,0:T(8,128)(2,1)S(1)} %copy-done.61, f32[3,512,512]{2,1,0:T(8,128)S(1)} %copy-done.51, ...), custom_call_target="tpu_custom_call" | custom-call | flops 7699999744 | bytes 65536 | tf_op jit(solution)/shard_map/pallas_call | solution.py:581
  160.7 3.4 %shard_map.259 = (bf16[2,512,256]{2,1,0:T(8,128)(2,1)S(1)}, bf16[2,512,256]{2,1,0:T(8,128)(2,1)S(1)}, f32[8,768]{1,0:T(8,128)}, bf16[208,768]{1,0:T(8,128)(2,1)S(1)}, bf16[208,768]{1,0:T(8,128)(2,1)}) custom-call(s32[2]{0:T(128)S(1)} %pad_add_fusion.1.refs_0_.meta, bf16[512,768]{1,0:T(8,128)(2,1)S(1)} %copy-done.18, f32[768]{0:T(1024)S(1)} %copy-done.32, ...), custom_call_target="tpu_custom_call" | custom-call | flops 4400000000 | bytes 65536 | tf_op jit(solution)/shard_map/pallas_call | solution.py:581
  165.6 1.1 collective-permute-start.41
  167.5 9.8 %collective-permute-done.41.got = bf16[208,768]{1,0:T(8,128)(2,1)} collective-permute-done((bf16[208,768]{1,0:T(8,128)(2,1)}, bf16[208,768]{1,0:T(8,128)(2,1)}, u32[]{:S(2)}, u32[]{:S(2)}) %collective-permute-start.41) | collective-permute-done | bytes 319520 | tf_op jit(solution)/shard_map/ppermute | solution.py:596
  177.3 1.0 copy-done.47
  178.2 1.1 shard_map.261
  180.1 1.3 collective-permute-start.28
  181.4 9.0 %collective-permute-done.42.got = bf16[112,768]{1,0:T(8,128)(2,1)S(1)} collective-permute-done((bf16[112,768]{1,0:T(8,128)(2,1)S(1)}, bf16[112,768]{1,0:T(8,128)(2,1)S(1)}, u32[]{:S(2)}, u32[]{:S(2)}) %collective-permute-start.42) | collective-permute-done | bytes 172064 | tf_op jit(solution)/shard_map/ppermute | solution.py:596
  192.0 1.2 collective-permute-start.40
  193.2 4.9 %convolution_bitcast_fusion.1 = f32[1,768,768]{2,1,0:T(8,128)} fusion(bf16[1024,768]{1,0:T(8,128)(2,1)} %get-tuple-element.144, bf16[1024,768]{1,0:T(8,128)(2,1)} %get-tuple-element.145), kind=kOutput, calls=%fused_computation.1 | convolution fusion | flops 1207959552 | bytes 5505024 | tf_op jit(solution)/shard_map/dot_general | solution.py:36
  198.1 2.8 %convolution_bitcast_fusion = f32[1,768,768]{2,1,0:T(8,128)} fusion(bf16[1024,768]{1,0:T(8,128)(2,1)S(1)} %copy-done.5, bf16[1024,768]{1,0:T(8,128)(2,1)S(1)} %copy-done.7), kind=kOutput, calls=%fused_computation | convolution fusion | flops 1207959552 | bytes 5505024 | tf_op jit(solution)/shard_map/dot_general | solution.py:36
  201.1 3.0 %collective-permute-start.46 = (bf16[48,768]{1,0:T(8,128)(2,1)S(1)}, bf16[48,768]{1,0:T(8,128)(2,1)S(1)}, u32[]{:S(2)}, u32[]{:S(2)}) collective-permute-start(bf16[48,768]{1,0:T(8,128)(2,1)S(1)} %get-tuple-element.130), channel_id=1, source_target_pairs={{0,16},{4,20},{8,24},{12,28},{16,0},{20,4},{24,8},{28,12},{1,17},{... | collective-permute-start | bytes 221192 | tf_op jit(solution)/shard_map/ppermute | solution.py:596
  204.1 4.5 %collective-permute-done.46 = bf16[48,768]{1,0:T(8,128)(2,1)S(1)} collective-permute-done((bf16[48,768]{1,0:T(8,128)(2,1)S(1)}, bf16[48,768]{1,0:T(8,128)(2,1)S(1)}, u32[]{:S(2)}, u32[]{:S(2)}) %collective-permute-start.46) | collective-permute-done | bytes 73760 | tf_op jit(solution)/shard_map/ppermute | solution.py:596
  210.5 3.8 %collective-permute-done.47.second = bf16[96,768]{1,0:T(8,128)(2,1)S(1)} collective-permute-done((bf16[96,768]{1,0:T(8,128)(2,1)S(1)}, bf16[96,768]{1,0:T(8,128)(2,1)S(1)}, u32[]{:S(2)}, u32[]{:S(2)}) %collective-permute-start.47) | collective-permute-done | bytes 147488 | tf_op jit(solution)/shard_map/ppermute | solution.py:596
  215.5 1.2 shard_map.255.rest_1_
  218.1 1.0 copy-done.43
  219.1 1.6 shard_map.260.rest_0_
  220.7 0.9 copy.35
  221.6 22.1 %all-reduce.3.cloned.1.call-done = (bf16[192,768]{1,0:T(8,128)(2,1)}, bf16[192,768]{1,0:T(8,128)(2,1)}) async-done(((bf16[192,768]{1,0:T(8,128)(2,1)}, bf16[192,768]{1,0:T(8,128)(2,1)}), (bf16[192,768]{1,0:T(8,128)(2,1)}, bf16[192,768]{1,0:T(8,128)(2,1)})) %all-reduce.3.cloned.1.call-update) | async-done | bytes 589840 | tf_op jit(solution)/shard_map/psum | solution.py:846
  243.7 1.0 copy-done.28
  244.6 1.0 copy-done.29
  245.6 2.4 shard_map.264
  (215 shorter events, 28.9 us)
Async XLA Ops:
  7.2 236.5 %all-reduce.3.cloned.1.call-start = ((), (), s32[]{:S(2)}) async-start(), calls=%async_computation | async-start | bytes 1179648 | tf_op jit(solution)/shard_map/psum | solution.py:846
  7.3 153.2 %copy-start.40 = (s32[2]{0:T(128)}, s32[2]{0:T(128)S(1)}, u32[]{:S(2)}) copy-start(s32[2]{0:T(128)S(1)} %pad_add_fusion.1.refs_0_.meta) | copy-start | bytes 28
  13.5 16.9 %collective-permute-start.4 = (bf16[400,768]{1,0:T(8,128)(2,1)S(1)}, bf16[400,768]{1,0:T(8,128)(2,1)S(1)}, u32[]{:S(2)}, u32[]{:S(2)}) collective-permute-start(bf16[400,768]{1,0:T(8,128)(2,1)S(1)} %get-tuple-element.81.w0), channel_id=1, source_target_pairs={{0,2},{1,3},{2,0},{3,1},{4,6},{5,7},{6,4},{7,5},{8,10},{9,11},{10,... | collective-permute-start | bytes 1843208 | tf_op jit(solution)/shard_map/ppermute | solution.py:596
  16.5 13.9 %collective-permute-start.3 = (bf16[400,768]{1,0:T(8,128)(2,1)S(1)}, bf16[400,768]{1,0:T(8,128)(2,1)S(1)}, u32[]{:S(2)}, u32[]{:S(2)}) collective-permute-start(bf16[400,768]{1,0:T(8,128)(2,1)S(1)} %get-tuple-element.81.w0), channel_id=1, source_target_pairs={{0,1},{1,0},{2,3},{3,2},{4,5},{5,4},{6,7},{7,6},{8,9},{9,8},{10,11... | collective-permute-start | bytes 1843208 | tf_op jit(solution)/shard_map/ppermute | solution.py:596
  16.6 11.3 %collective-permute-start.13 = (bf16[768,128]{1,0:T(8,128)(2,1)S(1)}, bf16[768,128]{1,0:T(8,128)(2,1)}, u32[]{:S(2)}, u32[]{:S(2)}) collective-permute-start(bf16[768,128]{1,0:T(8,128)(2,1)S(1)} %pad_maximum_fusion.2), channel_id=1, source_target_pairs={{0,4},{4,0},{8,12},{12,8},{16,20},{20,16},{24,28},{28,24},{1,5},{5... | collective-permute-start | bytes 589832 | tf_op jit(solution)/shard_map/ppermute | solution.py:596
  31.4 18.3 %copy-start.10 = (bf16[400,768]{1,0:T(8,128)(2,1)S(1)}, bf16[400,768]{1,0:T(8,128)(2,1)}, u32[]{:S(2)}) copy-start(bf16[400,768]{1,0:T(8,128)(2,1)} %copy-done.9) | copy-start | bytes 1843204
  31.4 18.4 %copy-start.12 = (bf16[400,768]{1,0:T(8,128)(2,1)S(1)}, bf16[400,768]{1,0:T(8,128)(2,1)}, u32[]{:S(2)}) copy-start(bf16[400,768]{1,0:T(8,128)(2,1)} %copy-done.11) | copy-start | bytes 1843204
  31.4 18.4 %copy-start.36 = (s32[512]{0:T(512)S(1)}, s32[512]{0:T(512)}, u32[]{:S(2)}) copy-start(s32[512]{0:T(512)} %route.7) | copy-start | bytes 6148
  31.4 18.4 %copy-start.38 = (s32[512]{0:T(512)S(1)}, s32[512]{0:T(512)}, u32[]{:S(2)}) copy-start(s32[512]{0:T(512)} %slot.5) | copy-start | bytes 6148
  32.4 6.2 %collective-permute-start.14 = (bf16[768,128]{1,0:T(8,128)(2,1)S(1)}, bf16[768,128]{1,0:T(8,128)(2,1)S(1)}, u32[]{:S(2)}, u32[]{:S(2)}) collective-permute-start(bf16[768,128]{1,0:T(8,128)(2,1)S(1)} %pad_maximum_fusion.3), channel_id=1, source_target_pairs={{0,8},{4,12},{8,0},{12,4},{16,24},{20,28},{24,16},{28,20},{1,9},{5... | collective-permute-start | bytes 589832 | tf_op jit(solution)/shard_map/ppermute | solution.py:596
  34.3 6.9 %collective-permute-start.1 = (bf16[192,512]{1,0:T(8,128)(2,1)S(1)}, bf16[192,512]{1,0:T(8,128)(2,1)S(1)}, u32[]{:S(2)}, u32[]{:S(2)}) collective-permute-start(bf16[192,512]{1,0:T(8,128)(2,1)S(1)} %copy-done.14), channel_id=1, source_target_pairs={{0,2},{1,3},{2,0},{3,1},{4,6},{5,7},{6,4},{7,5},{8,10},{9,11},{10,... | collective-permute-start | bytes 589832 | tf_op jit(solution)/shard_map/ppermute | solution.py:596
  35.8 13.9 %collective-permute-start.5 = (bf16[400,768]{1,0:T(8,128)(2,1)}, bf16[400,768]{1,0:T(8,128)(2,1)S(1)}, u32[]{:S(2)}, u32[]{:S(2)}) collective-permute-start(bf16[400,768]{1,0:T(8,128)(2,1)} %copy-done.9), channel_id=1, source_target_pairs={{0,1},{1,0},{2,3},{3,2},{4,5},{5,4},{6,7},{7,6},{8,9},{9,8},{10,11... | collective-permute-start | bytes 1843208 | tf_op jit(solution)/shard_map/ppermute | solution.py:596
  38.6 10.3 %collective-permute-start.15 = (bf16[768,128]{1,0:T(8,128)(2,1)S(1)}, bf16[768,128]{1,0:T(8,128)(2,1)S(1)}, u32[]{:S(2)}, u32[]{:S(2)}) collective-permute-start(bf16[768,128]{1,0:T(8,128)(2,1)S(1)} %pad_maximum_fusion.4), channel_id=1, source_target_pairs={{0,16},{4,20},{8,24},{12,28},{16,0},{20,4},{24,8},{28,12},{1,17},{... | collective-permute-start | bytes 589832 | tf_op jit(solution)/shard_map/ppermute | solution.py:596
  41.2 8.6 %collective-permute-start = (bf16[192,512]{1,0:T(8,128)(2,1)S(1)}, bf16[192,512]{1,0:T(8,128)(2,1)S(1)}, u32[]{:S(2)}, u32[]{:S(2)}) collective-permute-start(bf16[192,512]{1,0:T(8,128)(2,1)S(1)} %copy-done.14), channel_id=1, source_target_pairs={{0,1},{1,0},{2,3},{3,2},{4,5},{5,4},{6,7},{7,6},{8,9},{9,8},{10,11... | collective-permute-start | bytes 589832 | tf_op jit(solution)/shard_map/ppermute | solution.py:596
  41.2 8.6 %collective-permute-start.2 = (bf16[192,512]{1,0:T(8,128)(2,1)S(1)}, bf16[192,512]{1,0:T(8,128)(2,1)S(1)}, u32[]{:S(2)}, u32[]{:S(2)}) collective-permute-start(bf16[192,512]{1,0:T(8,128)(2,1)S(1)} %collective-permute-done.1.m2), channel_id=1, source_target_pairs={{0,1},{1,0},{2,3},{3,2},{4,5},{5,4},{6,7},{7,6},{8,9},{9,8},{10,11... | collective-permute-start | bytes 589832 | tf_op jit(solution)/shard_map/ppermute | solution.py:596
  57.2 80.8 %copy-start.44 = (f32[512,1]{1,0:T(8,128)}, f32[512,1]{1,0:T(8,128)S(1)}, u32[]{:S(2)}) copy-start(f32[512,1]{1,0:T(8,128)S(1)} %get-tuple-element.83.gate) | copy-start | bytes 6148
  57.2 18.7 %collective-permute-start.16 = (bf16[1536,128]{1,0:T(8,128)(2,1)}, bf16[1536,128]{1,0:T(8,128)(2,1)S(1)}, u32[]{:S(2)}, u32[]{:S(2)}) collective-permute-start(bf16[1536,128]{1,0:T(8,128)(2,1)} %shard_map.251.c0), channel_id=1, source_target_pairs={{0,2},{1,3},{2,0},{3,1},{4,6},{5,7},{6,4},{7,5},{8,10},{9,11},{10,... | collective-permute-start | bytes 1179656 | tf_op jit(solution)/shard_map/ppermute | solution.py:596
  58.3 5.6 %collective-permute-start.6 = (bf16[32,768]{1,0:T(8,128)(2,1)S(1)}, bf16[32,768]{1,0:T(8,128)(2,1)S(1)}, u32[]{:S(2)}, u32[]{:S(2)}) collective-permute-start(bf16[32,768]{1,0:T(8,128)(2,1)S(1)} %get-tuple-element.85), channel_id=1, source_target_pairs={{0,4},{4,0},{8,12},{12,8},{16,20},{20,16},{24,28},{28,24},{1,5},{5... | collective-permute-start | bytes 147464 | tf_op jit(solution)/shard_map/ppermute | solution.py:596
  59.8 5.9 %collective-permute-start.7 = (bf16[32,768]{1,0:T(8,128)(2,1)S(1)}, bf16[32,768]{1,0:T(8,128)(2,1)S(1)}, u32[]{:S(2)}, u32[]{:S(2)}) collective-permute-start(bf16[32,768]{1,0:T(8,128)(2,1)S(1)} %get-tuple-element.86), channel_id=1, source_target_pairs={{0,8},{4,12},{8,0},{12,4},{16,24},{20,28},{24,16},{28,20},{1,9},{5... | collective-permute-start | bytes 147464 | tf_op jit(solution)/shard_map/ppermute | solution.py:596
  60.5 8.7 %collective-permute-start.8 = (bf16[32,768]{1,0:T(8,128)(2,1)S(1)}, bf16[32,768]{1,0:T(8,128)(2,1)S(1)}, u32[]{:S(2)}, u32[]{:S(2)}) collective-permute-start(bf16[32,768]{1,0:T(8,128)(2,1)S(1)} %get-tuple-element.87), channel_id=1, source_target_pairs={{0,12},{4,8},{8,4},{12,0},{16,28},{20,24},{24,20},{28,16},{1,13},{... | collective-permute-start | bytes 147464 | tf_op jit(solution)/shard_map/ppermute | solution.py:596
  61.8 8.1 %collective-permute-start.9 = (bf16[32,768]{1,0:T(8,128)(2,1)S(1)}, bf16[32,768]{1,0:T(8,128)(2,1)S(1)}, u32[]{:S(2)}, u32[]{:S(2)}) collective-permute-start(bf16[32,768]{1,0:T(8,128)(2,1)S(1)} %get-tuple-element.88), channel_id=1, source_target_pairs={{0,16},{4,20},{8,24},{12,28},{16,0},{20,4},{24,8},{28,12},{1,17},{... | collective-permute-start | bytes 147464 | tf_op jit(solution)/shard_map/ppermute | solution.py:596
  63.9 6.7 %collective-permute-start.10 = (bf16[32,768]{1,0:T(8,128)(2,1)S(1)}, bf16[32,768]{1,0:T(8,128)(2,1)S(1)}, u32[]{:S(2)}, u32[]{:S(2)}) collective-permute-start(bf16[32,768]{1,0:T(8,128)(2,1)S(1)} %get-tuple-element.89), channel_id=1, source_target_pairs={{0,20},{4,16},{8,28},{12,24},{16,4},{20,0},{24,12},{28,8},{1,21},{... | collective-permute-start | bytes 147464 | tf_op jit(solution)/shard_map/ppermute | solution.py:596
  65.7 6.7 %collective-permute-start.11 = (bf16[32,768]{1,0:T(8,128)(2,1)S(1)}, bf16[32,768]{1,0:T(8,128)(2,1)S(1)}, u32[]{:S(2)}, u32[]{:S(2)}) collective-permute-start(bf16[32,768]{1,0:T(8,128)(2,1)S(1)} %get-tuple-element.90), channel_id=1, source_target_pairs={{0,24},{4,28},{8,16},{12,20},{16,8},{20,12},{24,0},{28,4},{1,25},{... | collective-permute-start | bytes 147464 | tf_op jit(solution)/shard_map/ppermute | solution.py:596
  69.2 6.8 %collective-permute-start.12 = (bf16[32,768]{1,0:T(8,128)(2,1)S(1)}, bf16[32,768]{1,0:T(8,128)(2,1)S(1)}, u32[]{:S(2)}, u32[]{:S(2)}) collective-permute-start(bf16[32,768]{1,0:T(8,128)(2,1)S(1)} %get-tuple-element.91), channel_id=1, source_target_pairs={{0,28},{4,24},{8,20},{12,16},{16,12},{20,8},{24,4},{28,0},{1,29},{... | collective-permute-start | bytes 147464 | tf_op jit(solution)/shard_map/ppermute | solution.py:596
  76.0 7.8 %collective-permute-start.18 = (bf16[256,768]{1,0:T(8,128)(2,1)S(1)}, bf16[256,768]{1,0:T(8,128)(2,1)S(1)}, u32[]{:S(2)}, u32[]{:S(2)}) collective-permute-start(bf16[256,768]{1,0:T(8,128)(2,1)S(1)} %shard_map.252.x0), channel_id=1, source_target_pairs={{0,2},{1,3},{2,0},{3,1},{4,6},{5,7},{6,4},{7,5},{8,10},{9,11},{10,... | collective-permute-start | bytes 1179656 | tf_op jit(solution)/shard_map/ppermute | solution.py:596
  77.0 6.9 %collective-permute-start.20 = (bf16[1536,128]{1,0:T(8,128)(2,1)S(1)}, bf16[1536,128]{1,0:T(8,128)(2,1)S(1)}, u32[]{:S(2)}, u32[]{:S(2)}) collective-permute-start(bf16[1536,128]{1,0:T(8,128)(2,1)S(1)} %copy-done.2), channel_id=1, source_target_pairs={{0,1},{1,0},{2,3},{3,2},{4,5},{5,4},{6,7},{7,6},{8,9},{9,8},{10,11... | collective-permute-start | bytes 1179656 | tf_op jit(solution)/shard_map/ppermute | solution.py:596
  77.0 6.9 %collective-permute-start.17 = (bf16[256,768]{1,0:T(8,128)(2,1)S(1)}, bf16[256,768]{1,0:T(8,128)(2,1)S(1)}, u32[]{:S(2)}, u32[]{:S(2)}) collective-permute-start(bf16[256,768]{1,0:T(8,128)(2,1)S(1)} %shard_map.252.x0), channel_id=1, source_target_pairs={{0,1},{1,0},{2,3},{3,2},{4,5},{5,4},{6,7},{7,6},{8,9},{9,8},{10,11... | collective-permute-start | bytes 1179656 | tf_op jit(solution)/shard_map/ppermute | solution.py:596
  77.5 6.4 %collective-permute-start.21 = (bf16[1536,128]{1,0:T(8,128)(2,1)S(1)}, bf16[1536,128]{1,0:T(8,128)(2,1)S(1)}, u32[]{:S(2)}, u32[]{:S(2)}) collective-permute-start(bf16[1536,128]{1,0:T(8,128)(2,1)S(1)} %collective-permute-done.16.refs_8_.c2), channel_id=1, source_target_pairs={{0,1},{1,0},{2,3},{3,2},{4,5},{5,4},{6,7},{7,6},{8,9},{9,8},{10,11... | collective-permute-start | bytes 1179656 | tf_op jit(solution)/shard_map/ppermute | solution.py:596
  83.9 1.7 collective-permute-start.19
  96.4 16.9 %copy-start.4 = (bf16[1024,768]{1,0:T(8,128)(2,1)}, bf16[1024,768]{1,0:T(8,128)(2,1)S(1)}, u32[]{:S(2)}) copy-start(bf16[1024,768]{1,0:T(8,128)(2,1)S(1)} %get-tuple-element.101.refs_0_) | copy-start | bytes 4718596
  96.4 2.4 collective-permute-start.22
  99.0 11.9 %collective-permute-start.23 = (bf16[208,1024]{1,0:T(8,128)(2,1)S(1)}, bf16[208,1024]{1,0:T(8,128)(2,1)S(1)}, u32[]{:S(2)}, u32[]{:S(2)}) collective-permute-start(bf16[208,1024]{1,0:T(8,128)(2,1)S(1)} %fusion.3), channel_id=1, source_target_pairs={{0,2},{1,3},{2,0},{3,1},{4,6},{5,7},{6,4},{7,5},{8,10},{9,11},{10,... | collective-permute-start | bytes 1277960 | tf_op jit(solution)/shard_map/ppermute | solution.py:596
  111.1 26.9 %copy-start.53 = (bf16[512,768]{1,0:T(8,128)(2,1)S(1)}, bf16[512,768]{1,0:T(8,128)(2,1)}, u32[]{:S(2)}) copy-start(bf16[512,768]{1,0:T(8,128)(2,1)} %copy-done.52) | copy-start | bytes 2359300
  113.3 23.2 %collective-permute-start.24 = (bf16[2,192,1024]{2,1,0:T(8,128)(2,1)S(1)}, bf16[2,192,1024]{2,1,0:T(8,128)(2,1)S(1)}, u32[]{:S(2)}, u32[]{:S(2)}) collective-permute-start(bf16[2,192,1024]{2,1,0:T(8,128)(2,1)S(1)} %get-tuple-element.105), channel_id=1, source_target_pairs={{0,1},{1,0},{2,3},{3,2},{4,5},{5,4},{6,7},{7,6},{8,9},{9,8},{10,11... | collective-permute-start | bytes 2359304 | tf_op jit(solution)/shard_map/ppermute | solution.py:596
  113.4 24.6 %copy-start.55 = (f32[512,8]{1,0:T(8,128)S(1)}, f32[512,8]{1,0:T(8,128)}, u32[]{:S(2)}) copy-start(f32[512,8]{1,0:T(8,128)} %copy-done.54) | copy-start | bytes 49156
  113.5 7.7 %collective-permute-start.35 = (bf16[208,128]{1,0:T(8,128)(2,1)S(1)}, bf16[208,128]{1,0:T(8,128)(2,1)S(1)}, u32[]{:S(2)}, u32[]{:S(2)}) collective-permute-start(bf16[208,128]{1,0:T(8,128)(2,1)S(1)} %get-tuple-element.164), channel_id=1, source_target_pairs={{0,28},{4,24},{8,20},{12,16},{16,12},{20,8},{24,4},{28,0},{1,29},{... | collective-permute-start | bytes 159752 | tf_op jit(solution)/shard_map/ppermute | solution.py:596
  114.3 7.0 %collective-permute-start.34 = (bf16[208,128]{1,0:T(8,128)(2,1)S(1)}, bf16[208,128]{1,0:T(8,128)(2,1)S(1)}, u32[]{:S(2)}, u32[]{:S(2)}) collective-permute-start(bf16[208,128]{1,0:T(8,128)(2,1)S(1)} %get-tuple-element.165), channel_id=1, source_target_pairs={{0,24},{4,28},{8,16},{12,20},{16,8},{20,12},{24,0},{28,4},{1,25},{... | collective-permute-start | bytes 159752 | tf_op jit(solution)/shard_map/ppermute | solution.py:596
  117.4 7.9 %collective-permute-start.33 = (bf16[208,128]{1,0:T(8,128)(2,1)S(1)}, bf16[208,128]{1,0:T(8,128)(2,1)S(1)}, u32[]{:S(2)}, u32[]{:S(2)}) collective-permute-start(bf16[208,128]{1,0:T(8,128)(2,1)S(1)} %get-tuple-element.166), channel_id=1, source_target_pairs={{0,20},{4,16},{8,28},{12,24},{16,4},{20,0},{24,12},{28,8},{1,21},{... | collective-permute-start | bytes 159752 | tf_op jit(solution)/shard_map/ppermute | solution.py:596
  117.4 8.7 %collective-permute-start.32 = (bf16[208,128]{1,0:T(8,128)(2,1)S(1)}, bf16[208,128]{1,0:T(8,128)(2,1)S(1)}, u32[]{:S(2)}, u32[]{:S(2)}) collective-permute-start(bf16[208,128]{1,0:T(8,128)(2,1)S(1)} %get-tuple-element.167), channel_id=1, source_target_pairs={{0,16},{4,20},{8,24},{12,28},{16,0},{20,4},{24,8},{28,12},{1,17},{... | collective-permute-start | bytes 159752 | tf_op jit(solution)/shard_map/ppermute | solution.py:596
  121.2 6.2 %collective-permute-start.31 = (bf16[208,128]{1,0:T(8,128)(2,1)S(1)}, bf16[208,128]{1,0:T(8,128)(2,1)S(1)}, u32[]{:S(2)}, u32[]{:S(2)}) collective-permute-start(bf16[208,128]{1,0:T(8,128)(2,1)S(1)} %get-tuple-element.168), channel_id=1, source_target_pairs={{0,12},{4,8},{8,4},{12,0},{16,28},{20,24},{24,20},{28,16},{1,13},{... | collective-permute-start | bytes 159752 | tf_op jit(solution)/shard_map/ppermute | solution.py:596
  121.3 6.2 %collective-permute-start.30 = (bf16[208,128]{1,0:T(8,128)(2,1)S(1)}, bf16[208,128]{1,0:T(8,128)(2,1)S(1)}, u32[]{:S(2)}, u32[]{:S(2)}) collective-permute-start(bf16[208,128]{1,0:T(8,128)(2,1)S(1)} %get-tuple-element.169), channel_id=1, source_target_pairs={{0,8},{4,12},{8,0},{12,4},{16,24},{20,28},{24,16},{28,20},{1,9},{5... | collective-permute-start | bytes 159752 | tf_op jit(solution)/shard_map/ppermute | solution.py:596
  125.3 4.1 %collective-permute-start.29 = (bf16[208,128]{1,0:T(8,128)(2,1)S(1)}, bf16[208,128]{1,0:T(8,128)(2,1)S(1)}, u32[]{:S(2)}, u32[]{:S(2)}) collective-permute-start(bf16[208,128]{1,0:T(8,128)(2,1)S(1)} %get-tuple-element.170), channel_id=1, source_target_pairs={{0,4},{4,0},{8,12},{12,8},{16,20},{20,16},{24,28},{28,24},{1,5},{5... | collective-permute-start | bytes 159752 | tf_op jit(solution)/shard_map/ppermute | solution.py:596
  130.6 5.9 %collective-permute-start.37 = (bf16[208,512]{1,0:T(8,128)(2,1)S(1)}, bf16[208,512]{1,0:T(8,128)(2,1)S(1)}, u32[]{:S(2)}, u32[]{:S(2)}) collective-permute-start(bf16[208,512]{1,0:T(8,128)(2,1)S(1)} %shard_map.256.r0), channel_id=1, source_target_pairs={{0,2},{1,3},{2,0},{3,1},{4,6},{5,7},{6,4},{7,5},{8,10},{9,11},{10,... | collective-permute-start | bytes 638984 | tf_op jit(solution)/shard_map/ppermute | solution.py:596
  131.2 6.1 %collective-permute-start.36 = (bf16[208,512]{1,0:T(8,128)(2,1)S(1)}, bf16[208,512]{1,0:T(8,128)(2,1)S(1)}, u32[]{:S(2)}, u32[]{:S(2)}) collective-permute-start(bf16[208,512]{1,0:T(8,128)(2,1)S(1)} %shard_map.256.r0), channel_id=1, source_target_pairs={{0,1},{1,0},{2,3},{3,2},{4,5},{5,4},{6,7},{7,6},{8,9},{9,8},{10,11... | collective-permute-start | bytes 638984 | tf_op jit(solution)/shard_map/ppermute | solution.py:596
  136.5 1.5 collective-permute-start.38
  136.7 22.6 %collective-permute-start.25 = (bf16[192,1024]{1,0:T(8,128)(2,1)S(1)}, bf16[192,1024]{1,0:T(8,128)(2,1)S(1)}, u32[]{:S(2)}, u32[]{:S(2)}) collective-permute-start(bf16[192,1024]{1,0:T(8,128)(2,1)S(1)} %fusion.5._), channel_id=1, source_target_pairs={{0,2},{1,3},{2,0},{3,1},{4,6},{5,7},{6,4},{7,5},{8,10},{9,11},{10,... | collective-permute-start | bytes 1179656 | tf_op jit(solution)/shard_map/ppermute | solution.py:596
  138.0 16.5 %copy-start.57 = (bf16[512,192]{1,0:T(8,128)(2,1)S(1)}, bf16[512,192]{1,0:T(8,128)(2,1)}, u32[]{:S(2)}) copy-start(bf16[512,192]{1,0:T(8,128)(2,1)} %copy-done.56) | copy-start | bytes 589828
  138.1 16.5 %copy-start.59 = (bf16[512,192]{1,0:T(8,128)(2,1)S(1)}, bf16[512,192]{1,0:T(8,128)(2,1)}, u32[]{:S(2)}) copy-start(bf16[512,192]{1,0:T(8,128)(2,1)} %copy-done.58) | copy-start | bytes 589828
  138.1 16.5 %copy-start.61 = (bf16[512,192]{1,0:T(8,128)(2,1)S(1)}, bf16[512,192]{1,0:T(8,128)(2,1)}, u32[]{:S(2)}) copy-start(bf16[512,192]{1,0:T(8,128)(2,1)} %copy-done.60) | copy-start | bytes 589828
  159.6 7.1 %collective-permute-start.26 = (bf16[768,128]{1,0:T(8,128)(2,1)S(1)}, bf16[768,128]{1,0:T(8,128)(2,1)S(1)}, u32[]{:S(2)}, u32[]{:S(2)}) collective-permute-start(bf16[768,128]{1,0:T(8,128)(2,1)S(1)} %pad_maximum_fusion.5), channel_id=1, source_target_pairs={{0,4},{4,0},{8,12},{12,8},{16,20},{20,16},{24,28},{28,24},{1,5},{5... | collective-permute-start | bytes 589832 | tf_op jit(solution)/shard_map/ppermute | solution.py:596
  165.6 11.7 %collective-permute-start.41 = (bf16[208,768]{1,0:T(8,128)(2,1)}, bf16[208,768]{1,0:T(8,128)(2,1)}, u32[]{:S(2)}, u32[]{:S(2)}) collective-permute-start(bf16[208,768]{1,0:T(8,128)(2,1)} %get-tuple-element.124), channel_id=1, source_target_pairs={{0,4},{4,0},{8,12},{12,8},{16,20},{20,16},{24,28},{28,24},{1,5},{5... | collective-permute-start | bytes 958472 | tf_op jit(solution)/shard_map/ppermute | solution.py:596
  167.4 12.0 %collective-permute-start.27 = (bf16[768,128]{1,0:T(8,128)(2,1)}, bf16[768,128]{1,0:T(8,128)(2,1)S(1)}, u32[]{:S(2)}, u32[]{:S(2)}) collective-permute-start(bf16[768,128]{1,0:T(8,128)(2,1)} %pad_maximum_fusion.6), channel_id=1, source_target_pairs={{0,8},{4,12},{8,0},{12,4},{16,24},{20,28},{24,16},{28,20},{1,9},{5... | collective-permute-start | bytes 589832 | tf_op jit(solution)/shard_map/ppermute | solution.py:596
  167.4 23.7 %collective-permute-start.39 = (bf16[2,512,256]{2,1,0:T(8,128)(2,1)}, bf16[2,512,256]{2,1,0:T(8,128)(2,1)S(1)}, u32[]{:S(2)}, u32[]{:S(2)}) collective-permute-start(bf16[2,512,256]{2,1,0:T(8,128)(2,1)} %copy-done.19), channel_id=1, source_target_pairs={{0,1},{1,0},{2,3},{3,2},{4,5},{5,4},{6,7},{7,6},{8,9},{9,8},{10,11... | collective-permute-start | bytes 1572872 | tf_op jit(solution)/shard_map/ppermute | solution.py:596
  179.3 11.1 %collective-permute-start.42 = (bf16[112,768]{1,0:T(8,128)(2,1)S(1)}, bf16[112,768]{1,0:T(8,128)(2,1)S(1)}, u32[]{:S(2)}, u32[]{:S(2)}) collective-permute-start(bf16[112,768]{1,0:T(8,128)(2,1)S(1)} %get-tuple-element.126), channel_id=1, source_target_pairs={{0,8},{4,12},{8,0},{12,4},{16,24},{20,28},{24,16},{28,20},{1,9},{5... | collective-permute-start | bytes 516104 | tf_op jit(solution)/shard_map/ppermute | solution.py:596
  180.1 28.7 %collective-permute-start.28 = (bf16[768,128]{1,0:T(8,128)(2,1)}, bf16[768,128]{1,0:T(8,128)(2,1)}, u32[]{:S(2)}, u32[]{:S(2)}) collective-permute-start(bf16[768,128]{1,0:T(8,128)(2,1)} %pad_maximum_fusion.7), channel_id=1, source_target_pairs={{0,16},{4,20},{8,24},{12,28},{16,0},{20,4},{24,8},{28,12},{1,17},{... | collective-permute-start | bytes 589832 | tf_op jit(solution)/shard_map/ppermute | solution.py:596
  191.1 9.8 %collective-permute-start.43 = (bf16[64,768]{1,0:T(8,128)(2,1)S(1)}, bf16[64,768]{1,0:T(8,128)(2,1)S(1)}, u32[]{:S(2)}, u32[]{:S(2)}) collective-permute-start(bf16[64,768]{1,0:T(8,128)(2,1)S(1)} %get-tuple-element.128), channel_id=1, source_target_pairs={{0,16},{4,20},{8,24},{12,28},{16,0},{20,4},{24,8},{28,12},{1,17},{... | collective-permute-start | bytes 294920 | tf_op jit(solution)/shard_map/ppermute | solution.py:596
  192.0 26.1 %collective-permute-start.40 = (bf16[512,256]{1,0:T(8,128)(2,1)}, bf16[512,256]{1,0:T(8,128)(2,1)}, u32[]{:S(2)}, u32[]{:S(2)}) collective-permute-start(bf16[512,256]{1,0:T(8,128)(2,1)} %get-tuple-element.162.refs_4_), channel_id=1, source_target_pairs={{0,2},{1,3},{2,0},{3,1},{4,6},{5,7},{6,4},{7,5},{8,10},{9,11},{10,... | collective-permute-start | bytes 786440 | tf_op jit(solution)/shard_map/ppermute | solution.py:596
  200.9 14.5 %copy-start.41 = (s32[2]{0:T(128)S(1)}, s32[2]{0:T(128)}, u32[]{:S(2)}) copy-start(s32[2]{0:T(128)} %copy-done.40) | copy-start | bytes 28
  200.9 14.5 %copy-start.45 = (f32[512,1]{1,0:T(8,128)S(1)}, f32[512,1]{1,0:T(8,128)}, u32[]{:S(2)}) copy-start(f32[512,1]{1,0:T(8,128)} %copy-done.44) | copy-start | bytes 6148
  201.0 8.7 %collective-permute-start.44 = (f32[8,768]{1,0:T(8,128)S(1)}, f32[8,768]{1,0:T(8,128)S(1)}, u32[]{:S(2)}, u32[]{:S(2)}) collective-permute-start(f32[8,768]{1,0:T(8,128)S(1)} %get-tuple-element.129), channel_id=1, source_target_pairs={{0,1},{1,0},{2,3},{3,2},{4,5},{5,4},{6,7},{7,6},{8,9},{9,8},{10,11... | collective-permute-start | bytes 73736 | tf_op jit(solution)/shard_map/ppermute | solution.py:596
  201.1 7.5 %collective-permute-start.46 = (bf16[48,768]{1,0:T(8,128)(2,1)S(1)}, bf16[48,768]{1,0:T(8,128)(2,1)S(1)}, u32[]{:S(2)}, u32[]{:S(2)}) collective-permute-start(bf16[48,768]{1,0:T(8,128)(2,1)S(1)} %get-tuple-element.130), channel_id=1, source_target_pairs={{0,16},{4,20},{8,24},{12,28},{16,0},{20,4},{24,8},{28,12},{1,17},{... | collective-permute-start | bytes 221192 | tf_op jit(solution)/shard_map/ppermute | solution.py:596
  208.5 5.7 %collective-permute-start.47 = (bf16[96,768]{1,0:T(8,128)(2,1)S(1)}, bf16[96,768]{1,0:T(8,128)(2,1)S(1)}, u32[]{:S(2)}, u32[]{:S(2)}) collective-permute-start(bf16[96,768]{1,0:T(8,128)(2,1)S(1)} %constant_dynamic-update-slice_fusion.mine), channel_id=1, source_target_pairs={{0,8},{4,12},{8,0},{12,4},{16,24},{20,28},{24,16},{28,20},{1,9},{5... | collective-permute-start | bytes 442376 | tf_op jit(solution)/shard_map/ppermute | solution.py:596
  209.7 7.8 %collective-permute-start.45 = (f32[8,768]{1,0:T(8,128)S(1)}, f32[8,768]{1,0:T(8,128)S(1)}, u32[]{:S(2)}, u32[]{:S(2)}) collective-permute-start(f32[8,768]{1,0:T(8,128)S(1)} %add.48), channel_id=1, source_target_pairs={{0,2},{1,3},{2,0},{3,1},{4,6},{5,7},{6,4},{7,5},{8,10},{9,11},{10,... | collective-permute-start | bytes 73736 | tf_op jit(solution)/shard_map/ppermute | solution.py:596
  215.0 28.7 %collective-permute-start.48 = (bf16[192,768]{1,0:T(8,128)(2,1)}, bf16[192,768]{1,0:T(8,128)(2,1)}, u32[]{:S(2)}, u32[]{:S(2)}) collective-permute-start(bf16[192,768]{1,0:T(8,128)(2,1)} %pad_maximum_fusion.1), channel_id=1, source_target_pairs={{0,4},{4,0},{8,12},{12,8},{16,20},{20,16},{24,28},{28,24},{1,5},{5... | collective-permute-start | bytes 884744 | tf_op jit(solution)/shard_map/ppermute | solution.py:596
  (49 other events, 148.4 us)
Sparse Core Ops, SparseCore 0:
  167.6 76.0 all-reduce.2
where the time goes:
time: 260 us; the launch traced here: 255 us
  waiting for transfers between devices  101 us (39%)
  Pallas kernels  53 us (20%)
  starting transfers between devices  46.3 us (18%)
  local copies, waits for them, and re-layouts  27.5 us (11%)
  between operations  14.8 us (6%)
  matrix products  7.73 us (3%)
  other arithmetic  4.66 us (2%)
    ppermute x49, waiting for transfers between devices, swap(): return lax.ppermute(array, axis, [(i, i ^ bit) for i in range(size)])  78.9 us
    pallas_call x16, Pallas kernels, call(): pl.pallas_call(kernel, out_shape=[jax.ShapeDtypeStruct(shape, kind) for s...  53 us
    ppermute x49, starting transfers between devices, swap(): return lax.ppermute(array, axis, [(i, i ^ bit) for i in range(size)])  46.3 us
    unnamed x129, local copies, waits for them, and re-layouts  24.8 us
    psum x1, waiting for transfers between devices, on_device(): first_grads = lax.psum(tuple(first_grads), 'expert')  22.1 us
    dot_general x2, matrix products, dot_tn(): lax.dot_general(a, b, (((0,), (0,)), ((), ())), precision=precision, pref...  7.73 us
  transfers between devices with their start and end apart: 50, of which 20 were waited for; matrix products, arithmetic and copies ran while one was open for 6% of the time, Pallas kernels for 13%

commit v1 on v0

--- a/solution.py
+++ b/solution.py
@@ -160,7 +160,7 @@
 
 
 def residual_kernel(
-    meta, route, slot, m0, m1, m2, m3, w0, w1, w2, w3, tokens,
+    meta, route, slot, tokens, m0, m1, m2, m3, w0, w1, w2, w3,
     residual_out, gate_out, probs_out, params_out, turned_out, *rest,
 ):
     outs, place, cot_place = rest[:-2], rest[-2], rest[-1]
@@ -308,12 +308,22 @@
     block_out[...] = (place[rank] + gate[...] * returned).astype(BF16)
 
 
+def put_chunks(grads, keep, send, place, expert, order):
+    count = len(order)
+    size = grads.shape[0] // count
+    for c in range(count):
+        place[c ^ expert] = grads[c * size : (c + 1) * size, :]
+    for i, k in enumerate(order):
+        out = keep if i < count // 2 else send
+        at = (i % (count // 2)) * size
+        out[at : at + size, :] = place[k]
+
+
 def residual_back_kernel(
     meta, r0, r1, r2, r3, residual, gate, probs, route, params, cotangent, mixed, w_attn_out,
     attn_probs, normed_one, _, d_attn_cols_out, d_mixed_out, d_value_out, router_grad_out,
-    gain_grad_out, *rest,
+    gain_grad_out, first_out, second_out, place, place_f32, chunk_place, *, chunked,
 ):
-    attn_grad_out, value_grad_out, place, place_f32 = rest
     rank, expert = meta[0], meta[1]
     experts = probs.shape[1]
     feats = residual.shape[1]
@@ -351,7 +361,7 @@
 
     d_attn_cols_out[...] = place_f32[rank]
     d_attn = d_residual.astype(BF16)
-    attn_grad_out[...] = dot_nn(mixed[...], d_attn).astype(BF16)
+    attn_grad = dot_nn(mixed[...], d_attn).astype(BF16)
     d_mixed = dot_nt(d_attn, w_attn_out[...]).astype(BF16)
     d_mixed_out[...] = d_mixed
     for h in range(cols // HDIM):
@@ -361,7 +371,13 @@
             span = slice(c, c + CHUNK)
             total = total + dot_tn(attn_probs[h, span, :].astype(BF16), d_mixed[span, own])
         d_value_out[:, own] = total.astype(BF16)
-    value_grad_out[...] = dot_tn(d_value_out[...], normed_one[...]).astype(BF16)
+    value_grad = dot_tn(d_value_out[...], normed_one[...]).astype(BF16)
+    if chunked:
+        both = jnp.concatenate([attn_grad, value_grad], axis=0)
+        put_chunks(both, first_out, second_out, chunk_place, expert, chunked)
+    else:
+        first_out[...] = attn_grad
+        second_out[...] = value_grad
 
 
 def attend_back_kernel(
@@ -405,7 +421,7 @@
 
 def query_back_kernel(
     meta, tokens, gain, normed, d_query, d_key, d_value, w_query, w_key, w_value, gain2_grad,
-    table_grad, router_grad, _, *rest, chunked, heads, buckets,
+    table_grad, router_grad, _, _got, *rest, chunked, heads, buckets,
 ):
     keep_in, send_in, gain1_out, first_out, second_out, place, chunk_place, pack = rest
     rank, expert = meta[0], meta[1]
@@ -433,14 +449,7 @@
             put_split(pack, 256 * (e % 3), 3 + e // 3, router_grad[e : e + 1, :])
         small = pack[...].astype(BF16)
         both = jnp.concatenate([query_grad, key_grad], axis=0)
-        count = len(chunked)
-        size = both.shape[0] // count
-        for c in range(count):
-            chunk_place[c ^ expert] = both[c * size : (c + 1) * size, :]
-        for i, k in enumerate(chunked):
-            out = first_out if i < count // 2 else second_out
-            at = (i % (count // 2)) * size
-            out[at : at + size, :] = chunk_place[k]
+        put_chunks(both, first_out, second_out, chunk_place, expert, chunked)
         for out in (first_out, second_out):
             out[out.shape[0] - 16 :, :] = small
     else:
@@ -513,12 +522,7 @@
     gain1_out[...] = jnp.broadcast_to(total[0:1], gain1_out.shape)
 
 
-def finish_kernel(
-    meta, mine, second, other, small, attn, value, *rest, order, heads
-):
-    attn_out, value_out, first_out, second_out, gain2_out, table_out, router_out, place = rest[-8:]
-    attn_out[...] = attn[...].astype(F32)
-    value_out[...] = value[...].astype(F32)
+def spread_kernel(meta, mine, second, other, first_out, second_out, place, *, order):
     expert = meta[1]
     count = len(order)
     size = mine.shape[0] // 2
@@ -538,6 +542,13 @@
             first_out[start : start + size, :] = chunk
         else:
             second_out[start - rows : start - rows + size, :] = chunk
+
+
+def finish_kernel(
+    meta, mine, second, other, small, *rest, order, heads
+):
+    first_out, second_out, gain2_out, table_out, router_out, place = rest[-6:]
+    spread_kernel(meta, mine, second, other, first_out, second_out, place, order=order)
     cols = gain2_out.shape[1]
     gain2_out[...] = small[1:2, :cols]
     for h in range(heads):
@@ -547,48 +558,72 @@
         router_out[e : e + 1, :] = small[3 + e // 3 : 4 + e // 3, at : at + cols]
 
 
-def fetching(kernel, smem, fetch):
+def moving(kernel, smem, fetch, total, far):
     def run(*refs):
-        scalars, far = refs[:smem], refs[smem : smem + fetch]
-        rest, near, sems = refs[smem + fetch : -fetch - 1], refs[-fetch - 1 : -1], refs[-1]
+        rest = list(refs[: len(refs) - 1])
+        sems = refs[-1]
+        near_out = rest[len(rest) - len(far) :] if far else []
+        rest = rest[: len(rest) - len(far)]
+        near_in = rest[len(rest) - fetch :] if fetch else []
+        rest = rest[: len(rest) - fetch]
         copies = [
-            pltpu.make_async_copy(a, b, sems.at[i]) for i, (a, b) in enumerate(zip(far, near))
+            pltpu.make_async_copy(rest[smem + i], b, sems.at[i]) for i, b in enumerate(near_in)
         ]
         for copy in copies:
             copy.start()
         for copy in copies:
             copy.wait()
-        kernel(*scalars, *near, *rest)
+        inner = list(rest)
+        for i, b in enumerate(near_in):
+            inner[smem + i] = b
+        for b, at in zip(near_out, far):
+            inner[total + at] = b
+        kernel(*inner)
+        copies = [
+            pltpu.make_async_copy(b, rest[total + at], sems.at[fetch + i])
+            for i, (b, at) in enumerate(zip(near_out, far))
+        ]
+        for copy in copies:
+            copy.start()
+        for copy in copies:
+            copy.wait()
 
     return run
 
 
-def call(kernel, outs, scratch, *operands, weight=1.0, smem=1, fetch=0, after=()):
-    specs = []
-    for i in range(len(operands)):
+def call(kernel, outs, scratch, *operands, weight=1.0, smem=1, fetch=0, far=(), after=()):
+    specs, given = [], []
+    for i, operand in enumerate(operands):
         if i < smem:
             specs.append(pl.BlockSpec(memory_space=pltpu.SMEM))
         elif i < smem + fetch:
             specs.append(pl.BlockSpec(memory_space=pltpu.HBM))
+            operand = pltpu.with_memory_space_constraint(operand, pltpu.HBM)
         else:
             specs.append(pl.BlockSpec(memory_space=pltpu.VMEM))
+        given.append(operand)
     specs += [pl.BlockSpec(memory_space=pl.ANY)] * len(after)
     scratch_shapes = [pltpu.VMEM(shape, kind) for shape, kind in scratch]
-    if fetch:
-        kernel = fetching(kernel, smem, fetch)
+    shapes, out_specs = [], []
+    for i, (shape, kind) in enumerate(outs):
+        shapes.append(pltpu.HBM(shape, kind) if i in far else jax.ShapeDtypeStruct(shape, kind))
+        out_specs.append(pl.BlockSpec(memory_space=pltpu.HBM if i in far else pltpu.VMEM))
+    if fetch or far:
+        kernel = moving(kernel, smem, fetch, len(operands) + len(after), far)
         scratch_shapes += [pltpu.VMEM(a.shape, a.dtype) for a in operands[smem : smem + fetch]]
-        scratch_shapes.append(pltpu.SemaphoreType.DMA((fetch,)))
+        scratch_shapes += [pltpu.VMEM(*outs[i]) for i in far]
+        scratch_shapes.append(pltpu.SemaphoreType.DMA((fetch + len(far),)))
     return pl.pallas_call(
         kernel,
-        out_shape=[jax.ShapeDtypeStruct(shape, kind) for shape, kind in outs],
+        out_shape=shapes,
         in_specs=specs,
-        out_specs=[pl.BlockSpec(memory_space=pltpu.VMEM)] * len(outs),
+        out_specs=out_specs,
         scratch_shapes=scratch_shapes,
-        compiler_params=pltpu.CompilerParams(vmem_limit_bytes=28 * 1024 * 1024),
+        compiler_params=pltpu.CompilerParams(vmem_limit_bytes=32 * 1024 * 1024),
         cost_estimate=pl.CostEstimate(
             flops=int(weight * 1.1e9), bytes_accessed=1 << 16, transcendentals=0
         ),
-    )(*operands, *after)
+    )(*given, *after)
 
 
 def swap(array, axis, bit):
@@ -618,7 +653,7 @@
     return [blocks[0]] + [swap(b, "expert", k) for k, b in enumerate(blocks) if k]
 
 
-def hyper_exchange(blocks, after=()):
+def hyper_exchange(blocks, gates=None):
     count = len(blocks)
     held = {k: [b] for k, b in enumerate(blocks)}
     steps = []
@@ -626,9 +661,11 @@
     while bit < count:
         away = [k for k in sorted(held) if k & bit]
         sent = jnp.concatenate([b for k in away for b in held[k]], axis=0)
+        if gates and bit in gates:
+            (sent,) = fence([sent], gates[bit])
         got = swap(sent, "expert", bit)
-        if bit == 1 and after:
-            (got,) = fence([got], after)
+        if gates and -bit in gates:
+            (got,) = fence([got], gates[-bit])
         steps.append(got)
         size = blocks[0].shape[0]
         at = 0
@@ -645,19 +682,42 @@
 ORDER = (0, 4, 2, 6, 1, 5, 3, 7)
 
 
+def gather_chunks(mine, gates=None):
+    held = swap(mine, "expert", 4)
+    if gates:
+        (held,) = fence([held], (gates[0],))
+    held = jnp.concatenate([mine, held], axis=0)
+    beside = swap(held, "expert", 2)
+    if gates:
+        (beside,) = fence([beside], (gates[1],))
+    return held, beside, swap(jnp.concatenate([held, beside], axis=0), "expert", 1)
+
+
+def halve_plain(keep, got, gates):
+    for bit, gate in zip((2, 4), gates):
+        half = keep.shape[0] // 2
+        sent = add_low(keep[half:], got[half:])
+        keep = add_low(keep[:half], got[:half])
+        (got,) = fence([swap(sent, "expert", bit)], (gate,))
+    return add_low(keep, got)
+
+
 def halve(keep, send):
     feats = keep.shape[1]
+    steps = []
     for bit in (1, 2):
         rows = (keep.shape[0] - 16) // 2 + 16
         keep, send = call(
             sum_kernel, [((rows, feats), BF16)] * 2, [], keep, swap(send, "expert", bit), smem=0
         )
-    return call(
+        steps.append(send)
+    last = call(
         last_sum_kernel,
         [((keep.shape[0] - 16, feats), BF16), ((8, feats), F32), ((8, feats), F32)],
         [],
         keep, swap(send, "expert", 4), smem=0,
     )
+    return last, steps
 
 
 def fence(arrays, after):
@@ -707,11 +767,10 @@
         + [((heads, length, length), F32), ((cols, length), BF16)],
         [((length, length), F32)],
         tokens, w_query.T, w_key.T, w_value.T, norm1_gain, segment, bucket, bias_table.T,
-        weight=7.0, smem=0, fetch=8,
+        weight=7.0, smem=0, fetch=8, far=(0, 1, 2, 3, 4),
     )
 
     mixed_parts = gather_four(mixed)
-    cot_arrived, _ = hyper_exchange(cot_blocks, (mixed, packed_parts[1], packed_parts[2]))
     residual, gate, router_probs, params, cot_turned, *row_blocks = call(
         residual_kernel,
         [
@@ -723,11 +782,13 @@
         ]
         + [((share, feats), BF16)] * experts,
         [((4, packed_rows - 2 * cols, cols), F32), ((4, cols, length), BF16)],
-        meta, route, slot, *mixed_parts, *packed_parts, tokens,
-        weight=5.8,
-    )
-    (cot_own,) = fence([jnp.concatenate(cot_arrived, axis=0)], (residual,))
-    cot_rows = gather_four(cot_own)
+        meta, route, slot, tokens, *mixed_parts, *packed_parts,
+        weight=5.8, fetch=3, far=(0, 1, 2, 4),
+    )
+    cot_arrived, _ = hyper_exchange(
+        cot_blocks, {2: (mixed, packed_parts[1], packed_parts[2]), -4: (residual,)}
+    )
+    cot_rows = gather_four(jnp.concatenate(cot_arrived, axis=0))
     arrived = exchange(row_blocks)
     groups = GROUPS if direct else 1
     group_size = experts // groups
@@ -770,7 +831,7 @@
              ((2, part_rows, count), BF16)],
             [(x_shape, BF16), (c_shape, BF16), ((4, part_rows, count), BF16)],
             meta, *row_groups[g], *cot_rows, w_in, w_out, params[:experts],
-            weight=10.0,
+            weight=10.0, far=(0, 1, 2, 3) if direct else (),
         )
         near, far, _ = reduce_four(keep, send)
         whole = add_low(near, far)
@@ -811,23 +872,6 @@
         weight=1.2,
     )
 
-    d_attn_cols, d_mixed, d_value, router_grad, gain2_grad, *first_grads = call(
-        residual_back_kernel,
-        [((length, cols), F32), ((length, cols), BF16), ((length, cols), BF16),
-         ((experts, cols), F32), ((1, cols), F32)] + [((cols, feats), BF16)] * 2,
-        [((4, cols, length), BF16), ((4, length, cols), F32)],
-        meta, *routed_parts, residual, gate, router_probs, route, params, cot_turned, mixed,
-        w_attn_out, probs, normed, after=(met_fwd,),
-        weight=8.0,
-    )
-    d_query, d_key, table_grad = call(
-        functools.partial(attend_back_kernel, buckets=buckets),
-        [((length, cols), BF16)] * 2 + [((8, 128), F32)],
-        [],
-        query, key, value, probs, d_mixed, bucket, smem=0,
-        weight=7.0,
-    )
-    wide = -(-(cols + 2) // 128) * 128
     if chunked:
         size = 2 * cols // experts
         grad_outs = [((experts // 2 * size + 16, feats), BF16)] * 2
@@ -835,15 +879,33 @@
     else:
         grad_outs = [((cols, feats), BF16)] * 2
         chunk_scratch = ((16, 128), BF16)
+    d_attn_cols, d_mixed, d_value, router_grad, gain2_grad, *first_grads = call(
+        functools.partial(residual_back_kernel, chunked=chunked),
+        [((length, cols), F32), ((length, cols), BF16), ((length, cols), BF16),
+         ((experts, cols), F32), ((1, cols), F32)]
+        + [((cols, feats), BF16)] * 2,
+        [((4, cols, length), BF16), ((4, length, cols), F32), chunk_scratch],
+        meta, *routed_parts, residual, gate, router_probs, route, params, cot_turned, mixed,
+        w_attn_out, probs, normed, after=(met_fwd,),
+        weight=8.0, far=(0,),
+    )
+    d_query, d_key, table_grad = call(
+        functools.partial(attend_back_kernel, buckets=buckets),
+        [((length, cols), BF16)] * 2 + [((8, 128), F32)],
+        [],
+        query, key, value, probs, d_mixed, bucket, smem=0,
+        weight=7.0,
+    )
+    wide = -(-(cols + 2) // 128) * 128
+    first_got = swap(first_grads[1], "expert", 1) if chunked else d_query
     keep_in, send_in, gain1_grad, *second_grads = call(
         functools.partial(query_back_kernel, chunked=chunked, heads=heads, buckets=buckets),
         [((2, length, wide), BF16)] * 2 + [((8, feats), F32)] + grad_outs,
         [((4, length, wide), BF16), chunk_scratch, ((16, feats), F32)],
         meta, tokens, norm1_gain, normed, d_query, d_key, d_value, w_query_t, w_key_t,
-        w_value_t, gain2_grad, table_grad, router_grad, after=(whole_fwd,),
+        w_value_t, gain2_grad, table_grad, router_grad, after=(whole_fwd, first_got),
         weight=4.0,
     )
-    first_grads = lax.psum(tuple(first_grads), "expert")
     near_in, far_in, met_in = reduce_four(keep_in, send_in)
     (input_grad,) = call(
         input_kernel,
@@ -857,26 +919,35 @@
     expert_out_grad = sum(dot_tn(kept[4 * g], kept[4 * g + 1]) for g in range(groups))
     expert_in_grad = sum(dot_tn(kept[4 * g + 2], kept[4 * g + 3]) for g in range(groups))
     if chunked:
-        mine, small, gain1_grad = halve(*second_grads)
-        held = jnp.concatenate([mine, swap(mine, "expert", 4)], axis=0)
-        beside = swap(held, "expert", 2)
-        other = swap(jnp.concatenate([held, beside], axis=0), "expert", 1)
+        (mine, small, gain1_grad), steps = halve(*second_grads)
+        second_chunks = gather_chunks(mine)
+        attn_grad, value_grad = call(
+            functools.partial(spread_kernel, order=ORDER),
+            [((cols, feats), F32)] * 2,
+            [chunk_scratch],
+            meta,
+            *gather_chunks(
+                halve_plain(first_grads[0], *fence([first_got], (keep_in,)), steps),
+                (mine, second_chunks[0]),
+            ),
+            weight=1.6,
+        )
         for bit in (1, 2):
             gain1_grad = gain1_grad + swap(gain1_grad, "tensor", bit)
-        attn_grad, value_grad, query_grad, key_grad, gain2_grad, table_grad, router_grad = call(
+        query_grad, key_grad, gain2_grad, table_grad, router_grad = call(
             functools.partial(finish_kernel, order=ORDER, heads=heads),
-            [((cols, feats), F32)] * 4
+            [((cols, feats), F32)] * 2
             + [((1, cols), F32), ((heads, buckets), F32), ((experts, cols), F32)],
             [chunk_scratch],
-            meta, held, beside, other, small, *first_grads,
-            weight=1.6, after=(input_grad, block_out, gain1_grad),
+            meta, *second_chunks, small,
+            weight=1.6, after=(input_grad, block_out, gain1_grad, attn_grad),
         )
     else:
         query_grad, key_grad, gain2_grad, table_grad, router_grad = lax.psum(
             (*second_grads, gain2_grad, table_grad[:heads, :buckets], router_grad), "expert"
         )
         gain1_grad = lax.psum(gain1_grad, ("expert", "tensor"))
-        attn_grad, value_grad = first_grads
+        attn_grad, value_grad = lax.psum(tuple(first_grads), "expert")
     return (
         block_out,
         input_grad,

time: 260 us -> 233 us (0.90)
  waiting for transfers between devices: 101 us -> 66.8 us
  between operations: 14.8 us -> 1.58 us
  starting transfers between devices: 46.3 us -> 58.5 us
  other arithmetic: 4.66 us -> 14.9 us
  local copies, waits for them, and re-layouts: 27.5 us -> 18.4 us
  Pallas kernels: 53 us -> 60.3 us
    psum x1 -> x0, waiting for transfers between devices: 22.1 us -> none  [on_device(): first_grads = lax.psum(tuple(first_grads), 'expert')]
    ppermute x49 -> x55, starting transfers between devices: 46.3 us -> 58.5 us  [swap(): return lax.ppermute(array, axis, [(i, i ^ bit) for i in range(size)])]
    ppermute x49 -> x55, waiting for transfers between devices: 78.9 us -> 66.8 us  [swap(): return lax.ppermute(array, axis, [(i, i ^ bit) for i in range(size)])]
    unnamed x129 -> x121, local copies, waits for them, and re-layouts: 24.8 us -> 14.2 us
    pallas_call x16 -> x17, Pallas kernels: 53 us -> 60.3 us  [call(): pl.pallas_call(kernel, out_shape=shapes, in_specs=specs, out_specs=out_sp...]
    convert_element_type x5 -> x8, other arithmetic: 1.55 us -> 6.23 us  [add_low(): return (a.astype(F32) + b.astype(F32)).astype(BF16)]
    concatenate x2 -> x4, other arithmetic: 1.51 us -> 5.11 us  [the longest x2 3.26 us: gather_chunks(): jnp.concatenate([held, beside], axis=0)]
  transfers between devices with their start and end apart: 50 -> 55, of which waited for: 20 -> 20; matrix products, arithmetic and copies ran while one was open for 6% -> 12% of each run, Pallas kernels for 13% -> 20%
where the time goes in v1:
time: 233 us; the launch traced here: 228 us
  waiting for transfers between devices  66.8 us (29%)
  Pallas kernels  60.3 us (26%)
  starting transfers between devices  58.5 us (25%)
  local copies, waits for them, and re-layouts  18.4 us (8%)
  other arithmetic  14.9 us (6%)
  matrix products  7.72 us (3%)
    ppermute x55, waiting for transfers between devices, swap(): return lax.ppermute(array, axis, [(i, i ^ bit) for i in range(size)])  66.8 us
    pallas_call x17, Pallas kernels, call(): pl.pallas_call(kernel, out_shape=shapes, in_specs=specs, out_specs=out_sp...  60.3 us
    ppermute x55, starting transfers between devices, swap(): return lax.ppermute(array, axis, [(i, i ^ bit) for i in range(size)])  58.5 us
    unnamed x121, local copies, waits for them, and re-layouts  14.2 us
    dot_general x2, matrix products, dot_tn(): lax.dot_general(a, b, (((0,), (0,)), ((), ())), precision=precision, pref...  7.72 us
    convert_element_type x8, other arithmetic, add_low(): return (a.astype(F32) + b.astype(F32)).astype(BF16)  6.23 us
  transfers between devices with their start and end apart: 55, of which 20 were waited for; matrix products, arithmetic and copies ran while one was open for 12% of the time, Pallas kernels for 20%

profile of v1, /device:TPU:0, one launch (start us, length us, event | category | flops | bytes accessed | tf_op | source)
XLA Modules:
  0.0 228.2 jit_solution(8662981050365689932)
XLA Ops:
  0.7 2.3 shard_map.248
  3.0 3.0 %collective-permute-start.4 = (bf16[400,768]{1,0:T(8,128)(2,1)S(1)}, bf16[400,768]{1,0:T(8,128)(2,1)S(1)}, u32[]{:S(2)}, u32[]{:S(2)}) collective-permute-start(bf16[400,768]{1,0:T(8,128)(2,1)S(1)} %get-tuple-element.81.refs_8_), channel_id=1, source_target_pairs={{0,2},{1,3},{2,0},{3,1},{4,6},{5,7},{6,4},{7,5},{8,10},{9,11},{10,... | collective-permute-start | bytes 1843208 | tf_op jit(solution)/shard_map/ppermute | solution.py:631
  6.1 1.6 collective-permute-start.13
  8.3 7.0 %shard_map.247 = (bf16[512,768]{1,0:T(8,128)(2,1)}, bf16[512,192]{1,0:T(8,128)(2,1)}, bf16[512,192]{1,0:T(8,128)(2,1)}, bf16[512,192]{1,0:T(8,128)(2,1)}, f32[3,...) custom-call(bf16[512,768]{1,0:T(8,128)(2,1)} %tokens.3, bf16[192,768]{1,0:T(8,128)(2,1)} %bitcast.45, ...), custom_call_target="tpu_custom_call" | custom-call | flops 7699999744 | bytes 65536 | tf_op jit(solution)/shard_map/pallas_call | solution.py:616
  15.9 4.8 %collective-permute-done.4.refs_10_.refs_3_ = bf16[400,768]{1,0:T(8,128)(2,1)S(1)} collective-permute-done((bf16[400,768]{1,0:T(8,128)(2,1)S(1)}, bf16[400,768]{1,0:T(8,128)(2,1)S(1)}, u32[]{:S(2)}, u32[]{:S(2)}) %collective-permute-start.4) | collective-permute-done | bytes 614432 | tf_op jit(solution)/shard_map/ppermute | solution.py:631
  22.5 2.1 collective-permute-start.14
  25.1 5.0 %collective-permute-done.14 = bf16[768,128]{1,0:T(8,128)(2,1)S(1)} collective-permute-done((bf16[768,128]{1,0:T(8,128)(2,1)}, bf16[768,128]{1,0:T(8,128)(2,1)S(1)}, u32[]{:S(2)}, u32[]{:S(2)}) %collective-permute-start.14) | collective-permute-done | bytes 196640 | tf_op jit(solution)/shard_map/ppermute | solution.py:631
  30.2 2.8 %collective-permute-start.15 = (bf16[768,128]{1,0:T(8,128)(2,1)S(1)}, bf16[768,128]{1,0:T(8,128)(2,1)S(1)}, u32[]{:S(2)}, u32[]{:S(2)}) collective-permute-start(bf16[768,128]{1,0:T(8,128)(2,1)S(1)} %pad_maximum_fusion.5), channel_id=1, source_target_pairs={{0,16},{4,20},{8,24},{12,28},{16,0},{20,4},{24,8},{28,12},{1,17},{... | collective-permute-start | bytes 589832 | tf_op jit(solution)/shard_map/ppermute | solution.py:631
  33.0 1.1 copy-done.9
  34.1 1.1 copy-done.11
  36.1 7.8 %shard_map.249 = (f32[512,768]{1,0:T(8,128)}, f32[512,1]{1,0:T(8,128)}, f32[512,8]{1,0:T(8,128)}, f32[16,768]{1,0:T(8,128)S(1)}, bf16[768,512]{1,0:T(8,128)(2,1)...) custom-call(s32[2]{0:T(128)S(1)} %pad_add_fusion.1.refs_0_.meta, ...), custom_call_target="tpu_custom_call" | custom-call | flops 6380000256 | bytes 65536 | tf_op jit(solution)/shard_map/pallas_call | solution.py:616
  45.5 1.6 collective-permute-start.16
  47.1 1.5 collective-permute-start.6
  48.6 1.6 collective-permute-start.7
  51.2 3.3 %collective-permute-start.10 = (bf16[32,768]{1,0:T(8,128)(2,1)S(1)}, bf16[32,768]{1,0:T(8,128)(2,1)S(1)}, u32[]{:S(2)}, u32[]{:S(2)}) collective-permute-start(bf16[32,768]{1,0:T(8,128)(2,1)S(1)} %get-tuple-element.89), channel_id=1, source_target_pairs={{0,20},{4,16},{8,28},{12,24},{16,4},{20,0},{24,12},{28,8},{1,21},{... | collective-permute-start | bytes 147464 | tf_op jit(solution)/shard_map/ppermute | solution.py:631
  54.5 1.8 collective-permute-start.11
  56.2 2.0 collective-permute-start.12
  58.3 2.2 collective-permute-done.10.refs_5_
  60.4 2.6 %collective-permute-done.12.refs_7_ = bf16[32,768]{1,0:T(8,128)(2,1)S(1)} collective-permute-done((bf16[32,768]{1,0:T(8,128)(2,1)S(1)}, bf16[32,768]{1,0:T(8,128)(2,1)S(1)}, u32[]{:S(2)}, u32[]{:S(2)}) %collective-permute-start.12) | collective-permute-done | bytes 49184 | tf_op jit(solution)/shard_map/ppermute | solution.py:631
  64.2 6.8 %collective-permute-done.18.refs_3_ = bf16[256,768]{1,0:T(8,128)(2,1)S(1)} collective-permute-done((bf16[256,768]{1,0:T(8,128)(2,1)S(1)}, bf16[256,768]{1,0:T(8,128)(2,1)S(1)}, u32[]{:S(2)}, u32[]{:S(2)}) %collective-permute-start.18) | collective-permute-done | bytes 393248 | tf_op jit(solution)/shard_map/ppermute | solution.py:631
  70.9 1.7 collective-permute-done.19.refs_4_
  72.6 9.6 %shard_map.253 = (bf16[1024,768]{1,0:T(8,128)(2,1)}, bf16[1024,768]{1,0:T(8,128)(2,1)}, bf16[1024,768]{1,0:T(8,128)(2,1)}, bf16[1024,768]{1,0:T(8,128)(2,1)}, bf...) custom-call(s32[2]{0:T(128)S(1)} %pad_add_fusion.1.refs_0_.meta, ...), custom_call_target="tpu_custom_call" | custom-call | flops 11000000512 | bytes 65536 | tf_op jit(solution)/shard_map/pallas_call | solution.py:616
  82.4 2.2 collective-permute-done.22
  85.4 11.3 %collective-permute-done.23 = bf16[208,1024]{1,0:T(8,128)(2,1)S(1)} collective-permute-done((bf16[208,1024]{1,0:T(8,128)(2,1)S(1)}, bf16[208,1024]{1,0:T(8,128)(2,1)S(1)}, u32[]{:S(2)}, u32[]{:S(2)}) %collective-permute-start.23) | collective-permute-done | bytes 426016 | tf_op jit(solution)/shard_map/ppermute | solution.py:631
  97.0 2.2 shard_map.254
  99.4 2.1 collective-permute-start.35
  101.5 2.1 collective-permute-start.34
  103.6 3.5 %collective-permute-start.32 = (bf16[208,128]{1,0:T(8,128)(2,1)S(1)}, bf16[208,128]{1,0:T(8,128)(2,1)S(1)}, u32[]{:S(2)}, u32[]{:S(2)}) collective-permute-start(bf16[208,128]{1,0:T(8,128)(2,1)S(1)} %get-tuple-element.167), channel_id=1, source_target_pairs={{0,16},{4,20},{8,24},{12,28},{16,0},{20,4},{24,8},{28,12},{1,17},{... | collective-permute-start | bytes 159752 | tf_op jit(solution)/shard_map/ppermute | solution.py:631
  107.8 2.2 collective-permute-start.30
  110.0 1.7 collective-permute-done.33.rest_5_
  111.7 1.4 collective-permute-start.29
  113.8 2.0 collective-permute-done.29.rest_1_
  115.9 1.2 shard_map.256.refs_1_
  117.7 5.3 %collective-permute-done.37.refs_3_ = bf16[208,512]{1,0:T(8,128)(2,1)S(1)} collective-permute-done((bf16[208,512]{1,0:T(8,128)(2,1)S(1)}, bf16[208,512]{1,0:T(8,128)(2,1)S(1)}, u32[]{:S(2)}, u32[]{:S(2)}) %collective-permute-start.37) | collective-permute-done | bytes 213024 | tf_op jit(solution)/shard_map/ppermute | solution.py:631
  124.6 16.9 %shard_map.257 = (f32[512,192]{1,0:T(8,128)}, bf16[512,192]{1,0:T(8,128)(2,1)S(1)}, bf16[512,192]{1,0:T(8,128)(2,1)S(1)}, f32[8,192]{1,0:T(8,128)S(1)}, f32[1,19...) custom-call(s32[2]{0:T(128)S(1)} %pad_add_fusion.1.refs_0_.meta, ...), custom_call_target="tpu_custom_call" | custom-call | flops 8800000000 | bytes 65536 | tf_op jit(solution)/shard_map/pallas_call | solution.py:616
  141.5 1.5 collective-permute-start.39
  143.0 4.8 %shard_map.258 = (bf16[512,192]{1,0:T(8,128)(2,1)S(1)}, bf16[512,192]{1,0:T(8,128)(2,1)S(1)}, f32[8,128]{1,0:T(8,128)S(1)}) custom-call(bf16[512,192]{1,0:T(8,128)(2,1)S(1)} %copy-done.47, bf16[512,192]{1,0:T(8,128)(2,1)S(1)} %copy-done.48, bf16[512,192]{1,0:T(8,128)(2,1)S(1)} %copy-done.49, f32[3,512,512]{2,1,0:T(8,128)S(1)} %copy-done.43, ...), custom_call_target="tpu_custom_call" | custom-call | flops 7699999744 | bytes 65536 | tf_op jit(solution)/shard_map/pallas_call | solution.py:616
  149.4 1.3 collective-permute-done.39._got.refs_0_
  150.7 2.9 %shard_map.259 = (bf16[2,512,256]{2,1,0:T(8,128)(2,1)S(1)}, bf16[2,512,256]{2,1,0:T(8,128)(2,1)S(1)}, f32[8,768]{1,0:T(8,128)}, bf16[208,768]{1,0:T(8,128)(2,1)S(1)}, bf16[208,768]{1,0:T(8,128)(2,1)S(1)}) custom-call(s32[2]{0:T(128)S(1)} %pad_add_fusion.1.refs_0_.meta, bf16[512,768]{1,0:T(8,128)(2,1)S(1)} %copy-done.24, f32[768]{0:T(1024)S(1)} %copy-done.32, ...), custom_call_target="tpu_custom_call" | custom-call | flops 4400000000 | bytes 65536 | tf_op jit(solution)/shard_map/pallas_call | solution.py:616
  155.9 1.8 add_convert_fusion.7
  157.6 1.4 collective-permute-start.42
  160.7 2.0 collective-permute-start.27
  162.7 3.7 %collective-permute-done.42.got = bf16[208,768]{1,0:T(8,128)(2,1)S(1)} collective-permute-done((bf16[208,768]{1,0:T(8,128)(2,1)S(1)}, bf16[208,768]{1,0:T(8,128)(2,1)S(1)}, u32[]{:S(2)}, u32[]{:S(2)}) %collective-permute-start.42) | collective-permute-done | bytes 319520 | tf_op jit(solution)/shard_map/ppermute | solution.py:631
  166.5 1.8 collective-permute-start.43
  171.6 2.2 collective-permute-start.28
  175.5 7.8 %collective-permute-done.51.refs_0_ = bf16[48,768]{1,0:T(8,128)(2,1)} collective-permute-done((bf16[48,768]{1,0:T(8,128)(2,1)S(1)}, bf16[48,768]{1,0:T(8,128)(2,1)}, u32[]{:S(2)}, u32[]{:S(2)}) %collective-permute-start.51) | collective-permute-done | bytes 73760 | tf_op jit(solution)/shard_map/ppermute | solution.py:631
  183.3 1.0 add_convert_fusion.8
  184.4 1.9 fusion.7
  187.3 4.9 %convolution_bitcast_fusion.1 = f32[1,768,768]{2,1,0:T(8,128)} fusion(bf16[1024,768]{1,0:T(8,128)(2,1)} %get-tuple-element.144, bf16[1024,768]{1,0:T(8,128)(2,1)} %get-tuple-element.145), kind=kOutput, calls=%fused_computation.1 | convolution fusion | flops 1207959552 | bytes 5505024 | tf_op jit(solution)/shard_map/dot_general | solution.py:36
  192.2 2.8 %convolution_bitcast_fusion = f32[1,768,768]{2,1,0:T(8,128)} fusion(bf16[1024,768]{1,0:T(8,128)(2,1)S(1)} %copy-done.4, bf16[1024,768]{1,0:T(8,128)(2,1)S(1)} %copy-done.50), kind=kOutput, calls=%fused_computation | convolution fusion | flops 1207959552 | bytes 5505024 | tf_op jit(solution)/shard_map/dot_general | solution.py:36
  195.1 3.0 %collective-permute-start.47 = (bf16[48,768]{1,0:T(8,128)(2,1)S(1)}, bf16[48,768]{1,0:T(8,128)(2,1)S(1)}, u32[]{:S(2)}, u32[]{:S(2)}) collective-permute-start(bf16[48,768]{1,0:T(8,128)(2,1)S(1)} %get-tuple-element.131.refs_1_), channel_id=1, source_target_pairs={{0,16},{4,20},{8,24},{12,28},{16,0},{20,4},{24,8},{28,12},{1,17},{... | collective-permute-start | bytes 221192 | tf_op jit(solution)/shard_map/ppermute | solution.py:631
  201.5 1.1 collective-permute-start.46
  202.7 2.1 collective-permute-start.48
  205.7 1.2 shard_map.255.rest_1_
  208.4 1.6 pad_maximum_fusion.2
  210.1 2.2 collective-permute-start.54
  212.3 1.6 pad_maximum_fusion.1
  214.5 1.0 copy-done.36
  215.6 1.1 shard_map.260.rest_0_
  217.6 2.8 %collective-permute-done.54.other = bf16[192,768]{1,0:T(8,128)(2,1)S(1)} collective-permute-done((bf16[192,768]{1,0:T(8,128)(2,1)}, bf16[192,768]{1,0:T(8,128)(2,1)S(1)}, u32[]{:S(2)}, u32[]{:S(2)}) %collective-permute-start.54) | collective-permute-done | bytes 294944 | tf_op jit(solution)/shard_map/ppermute | solution.py:631
  220.4 1.6 shard_map.269
  222.0 3.3 %collective-permute-done.49.other = bf16[192,768]{1,0:T(8,128)(2,1)S(1)} collective-permute-done((bf16[192,768]{1,0:T(8,128)(2,1)}, bf16[192,768]{1,0:T(8,128)(2,1)S(1)}, u32[]{:S(2)}, u32[]{:S(2)}) %collective-permute-start.49) | collective-permute-done | bytes 294944 | tf_op jit(solution)/shard_map/ppermute | solution.py:631
  225.3 1.1 copy-done.35
  226.4 1.6 shard_map.270
  (227 shorter events, 32.2 us)
Async XLA Ops:
  3.0 17.7 %collective-permute-start.4 = (bf16[400,768]{1,0:T(8,128)(2,1)S(1)}, bf16[400,768]{1,0:T(8,128)(2,1)S(1)}, u32[]{:S(2)}, u32[]{:S(2)}) collective-permute-start(bf16[400,768]{1,0:T(8,128)(2,1)S(1)} %get-tuple-element.81.refs_8_), channel_id=1, source_target_pairs={{0,2},{1,3},{2,0},{3,1},{4,6},{5,7},{6,4},{7,5},{8,10},{9,11},{10,... | collective-permute-start | bytes 1843208 | tf_op jit(solution)/shard_map/ppermute | solution.py:631
  6.0 15.4 %collective-permute-start.3 = (bf16[400,768]{1,0:T(8,128)(2,1)S(1)}, bf16[400,768]{1,0:T(8,128)(2,1)S(1)}, u32[]{:S(2)}, u32[]{:S(2)}) collective-permute-start(bf16[400,768]{1,0:T(8,128)(2,1)S(1)} %get-tuple-element.81.refs_8_), channel_id=1, source_target_pairs={{0,1},{1,0},{2,3},{3,2},{4,5},{5,4},{6,7},{7,6},{8,9},{9,8},{10,11... | collective-permute-start | bytes 1843208 | tf_op jit(solution)/shard_map/ppermute | solution.py:631
  6.1 9.8 %collective-permute-start.13 = (bf16[768,128]{1,0:T(8,128)(2,1)S(1)}, bf16[768,128]{1,0:T(8,128)(2,1)S(1)}, u32[]{:S(2)}, u32[]{:S(2)}) collective-permute-start(bf16[768,128]{1,0:T(8,128)(2,1)S(1)} %pad_maximum_fusion.3), channel_id=1, source_target_pairs={{0,4},{4,0},{8,12},{12,8},{16,20},{20,16},{24,28},{28,24},{1,5},{5... | collective-permute-start | bytes 589832 | tf_op jit(solution)/shard_map/ppermute | solution.py:631
  15.3 9.3 %collective-permute-start.1 = (bf16[192,512]{1,0:T(8,128)(2,1)S(1)}, bf16[192,512]{1,0:T(8,128)(2,1)S(1)}, u32[]{:S(2)}, u32[]{:S(2)}) collective-permute-start(bf16[192,512]{1,0:T(8,128)(2,1)S(1)} %get-tuple-element.80.refs_4_.refs_1_.refs_11_), channel_id=1, source_target_pairs={{0,2},{1,3},{2,0},{3,1},{4,6},{5,7},{6,4},{7,5},{8,10},{9,11},{10,... | collective-permute-start | bytes 589832 | tf_op jit(solution)/shard_map/ppermute | solution.py:631
  20.7 12.3 %collective-permute-start.5 = (bf16[400,768]{1,0:T(8,128)(2,1)S(1)}, bf16[400,768]{1,0:T(8,128)(2,1)S(1)}, u32[]{:S(2)}, u32[]{:S(2)}) collective-permute-start(bf16[400,768]{1,0:T(8,128)(2,1)S(1)} %collective-permute-done.4.refs_10_.refs_3_), channel_id=1, source_target_pairs={{0,1},{1,0},{2,3},{3,2},{4,5},{5,4},{6,7},{7,6},{8,9},{9,8},{10,11... | collective-permute-start | bytes 1843208 | tf_op jit(solution)/shard_map/ppermute | solution.py:631
  22.5 7.7 %collective-permute-start.14 = (bf16[768,128]{1,0:T(8,128)(2,1)}, bf16[768,128]{1,0:T(8,128)(2,1)S(1)}, u32[]{:S(2)}, u32[]{:S(2)}) collective-permute-start(bf16[768,128]{1,0:T(8,128)(2,1)} %shard_map.250), channel_id=1, source_target_pairs={{0,8},{4,12},{8,0},{12,4},{16,24},{20,28},{24,16},{28,20},{1,9},{5... | collective-permute-start | bytes 589832 | tf_op jit(solution)/shard_map/ppermute | solution.py:631
  24.6 8.4 %collective-permute-start = (bf16[192,512]{1,0:T(8,128)(2,1)}, bf16[192,512]{1,0:T(8,128)(2,1)S(1)}, u32[]{:S(2)}, u32[]{:S(2)}) collective-permute-start(bf16[192,512]{1,0:T(8,128)(2,1)} %copy-done.16), channel_id=1, source_target_pairs={{0,1},{1,0},{2,3},{3,2},{4,5},{5,4},{6,7},{7,6},{8,9},{9,8},{10,11... | collective-permute-start | bytes 589832 | tf_op jit(solution)/shard_map/ppermute | solution.py:631
  24.6 8.4 %collective-permute-start.2 = (bf16[192,512]{1,0:T(8,128)(2,1)S(1)}, bf16[192,512]{1,0:T(8,128)(2,1)S(1)}, u32[]{:S(2)}, u32[]{:S(2)}) collective-permute-start(bf16[192,512]{1,0:T(8,128)(2,1)S(1)} %collective-permute-done.1.refs_6_), channel_id=1, source_target_pairs={{0,1},{1,0},{2,3},{3,2},{4,5},{5,4},{6,7},{7,6},{8,9},{9,8},{10,11... | collective-permute-start | bytes 589832 | tf_op jit(solution)/shard_map/ppermute | solution.py:631
  30.2 13.7 %collective-permute-start.15 = (bf16[768,128]{1,0:T(8,128)(2,1)S(1)}, bf16[768,128]{1,0:T(8,128)(2,1)S(1)}, u32[]{:S(2)}, u32[]{:S(2)}) collective-permute-start(bf16[768,128]{1,0:T(8,128)(2,1)S(1)} %pad_maximum_fusion.5), channel_id=1, source_target_pairs={{0,16},{4,20},{8,24},{12,28},{16,0},{20,4},{24,8},{28,12},{1,17},{... | collective-permute-start | bytes 589832 | tf_op jit(solution)/shard_map/ppermute | solution.py:631
  45.5 17.5 %collective-permute-start.16 = (bf16[1536,128]{1,0:T(8,128)(2,1)S(1)}, bf16[1536,128]{1,0:T(8,128)(2,1)S(1)}, u32[]{:S(2)}, u32[]{:S(2)}) collective-permute-start(bf16[1536,128]{1,0:T(8,128)(2,1)S(1)} %pad_maximum_fusion.refs_5_), channel_id=1, source_target_pairs={{0,2},{1,3},{2,0},{3,1},{4,6},{5,7},{6,4},{7,5},{8,10},{9,11},{10,... | collective-permute-start | bytes 1179656 | tf_op jit(solution)/shard_map/ppermute | solution.py:631
  47.1 4.1 %collective-permute-start.6 = (bf16[32,768]{1,0:T(8,128)(2,1)S(1)}, bf16[32,768]{1,0:T(8,128)(2,1)S(1)}, u32[]{:S(2)}, u32[]{:S(2)}) collective-permute-start(bf16[32,768]{1,0:T(8,128)(2,1)S(1)} %get-tuple-element.85), channel_id=1, source_target_pairs={{0,4},{4,0},{8,12},{12,8},{16,20},{20,16},{24,28},{28,24},{1,5},{5... | collective-permute-start | bytes 147464 | tf_op jit(solution)/shard_map/ppermute | solution.py:631
  48.6 5.9 %collective-permute-start.7 = (bf16[32,768]{1,0:T(8,128)(2,1)S(1)}, bf16[32,768]{1,0:T(8,128)(2,1)S(1)}, u32[]{:S(2)}, u32[]{:S(2)}) collective-permute-start(bf16[32,768]{1,0:T(8,128)(2,1)S(1)} %get-tuple-element.86), channel_id=1, source_target_pairs={{0,8},{4,12},{8,0},{12,4},{16,24},{20,28},{24,16},{28,20},{1,9},{5... | collective-permute-start | bytes 147464 | tf_op jit(solution)/shard_map/ppermute | solution.py:631
  50.2 6.1 %collective-permute-start.8 = (bf16[32,768]{1,0:T(8,128)(2,1)S(1)}, bf16[32,768]{1,0:T(8,128)(2,1)S(1)}, u32[]{:S(2)}, u32[]{:S(2)}) collective-permute-start(bf16[32,768]{1,0:T(8,128)(2,1)S(1)} %get-tuple-element.87), channel_id=1, source_target_pairs={{0,12},{4,8},{8,4},{12,0},{16,28},{20,24},{24,20},{28,16},{1,13},{... | collective-permute-start | bytes 147464 | tf_op jit(solution)/shard_map/ppermute | solution.py:631
  50.6 7.7 %collective-permute-start.9 = (bf16[32,768]{1,0:T(8,128)(2,1)S(1)}, bf16[32,768]{1,0:T(8,128)(2,1)S(1)}, u32[]{:S(2)}, u32[]{:S(2)}) collective-permute-start(bf16[32,768]{1,0:T(8,128)(2,1)S(1)} %get-tuple-element.88), channel_id=1, source_target_pairs={{0,16},{4,20},{8,24},{12,28},{16,0},{20,4},{24,8},{28,12},{1,17},{... | collective-permute-start | bytes 147464 | tf_op jit(solution)/shard_map/ppermute | solution.py:631
  51.2 9.2 %collective-permute-start.10 = (bf16[32,768]{1,0:T(8,128)(2,1)S(1)}, bf16[32,768]{1,0:T(8,128)(2,1)S(1)}, u32[]{:S(2)}, u32[]{:S(2)}) collective-permute-start(bf16[32,768]{1,0:T(8,128)(2,1)S(1)} %get-tuple-element.89), channel_id=1, source_target_pairs={{0,20},{4,16},{8,28},{12,24},{16,4},{20,0},{24,12},{28,8},{1,21},{... | collective-permute-start | bytes 147464 | tf_op jit(solution)/shard_map/ppermute | solution.py:631
  54.5 6.0 %collective-permute-start.11 = (bf16[32,768]{1,0:T(8,128)(2,1)S(1)}, bf16[32,768]{1,0:T(8,128)(2,1)S(1)}, u32[]{:S(2)}, u32[]{:S(2)}) collective-permute-start(bf16[32,768]{1,0:T(8,128)(2,1)S(1)} %get-tuple-element.90), channel_id=1, source_target_pairs={{0,24},{4,28},{8,16},{12,20},{16,8},{20,12},{24,0},{28,4},{1,25},{... | collective-permute-start | bytes 147464 | tf_op jit(solution)/shard_map/ppermute | solution.py:631
  56.2 6.8 %collective-permute-start.12 = (bf16[32,768]{1,0:T(8,128)(2,1)S(1)}, bf16[32,768]{1,0:T(8,128)(2,1)S(1)}, u32[]{:S(2)}, u32[]{:S(2)}) collective-permute-start(bf16[32,768]{1,0:T(8,128)(2,1)S(1)} %get-tuple-element.91), channel_id=1, source_target_pairs={{0,28},{4,24},{8,20},{12,16},{16,12},{20,8},{24,4},{28,0},{1,29},{... | collective-permute-start | bytes 147464 | tf_op jit(solution)/shard_map/ppermute | solution.py:631
  63.1 7.8 %collective-permute-start.18 = (bf16[256,768]{1,0:T(8,128)(2,1)S(1)}, bf16[256,768]{1,0:T(8,128)(2,1)S(1)}, u32[]{:S(2)}, u32[]{:S(2)}) collective-permute-start(bf16[256,768]{1,0:T(8,128)(2,1)S(1)} %shard_map.252.refs_1_), channel_id=1, source_target_pairs={{0,2},{1,3},{2,0},{3,1},{4,6},{5,7},{6,4},{7,5},{8,10},{9,11},{10,... | collective-permute-start | bytes 1179656 | tf_op jit(solution)/shard_map/ppermute | solution.py:631
  63.6 7.3 %collective-permute-start.20 = (bf16[1536,128]{1,0:T(8,128)(2,1)S(1)}, bf16[1536,128]{1,0:T(8,128)(2,1)S(1)}, u32[]{:S(2)}, u32[]{:S(2)}) collective-permute-start(bf16[1536,128]{1,0:T(8,128)(2,1)S(1)} %pad_maximum_fusion.refs_5_), channel_id=1, source_target_pairs={{0,1},{1,0},{2,3},{3,2},{4,5},{5,4},{6,7},{7,6},{8,9},{9,8},{10,11... | collective-permute-start | bytes 1179656 | tf_op jit(solution)/shard_map/ppermute | solution.py:631
  63.6 7.3 %collective-permute-start.17 = (bf16[256,768]{1,0:T(8,128)(2,1)S(1)}, bf16[256,768]{1,0:T(8,128)(2,1)S(1)}, u32[]{:S(2)}, u32[]{:S(2)}) collective-permute-start(bf16[256,768]{1,0:T(8,128)(2,1)S(1)} %shard_map.252.refs_1_), channel_id=1, source_target_pairs={{0,1},{1,0},{2,3},{3,2},{4,5},{5,4},{6,7},{7,6},{8,9},{9,8},{10,11... | collective-permute-start | bytes 1179656 | tf_op jit(solution)/shard_map/ppermute | solution.py:631
  64.2 6.8 %collective-permute-start.21 = (bf16[1536,128]{1,0:T(8,128)(2,1)S(1)}, bf16[1536,128]{1,0:T(8,128)(2,1)S(1)}, u32[]{:S(2)}, u32[]{:S(2)}) collective-permute-start(bf16[1536,128]{1,0:T(8,128)(2,1)S(1)} %collective-permute-done.16.refs_8_.refs_7_), channel_id=1, source_target_pairs={{0,1},{1,0},{2,3},{3,2},{4,5},{5,4},{6,7},{7,6},{8,9},{9,8},{10,11... | collective-permute-start | bytes 1179656 | tf_op jit(solution)/shard_map/ppermute | solution.py:631
  70.9 1.7 collective-permute-start.19
  82.2 2.4 %collective-permute-start.22 = (bf16[2,208,1024]{2,1,0:T(8,128)(2,1)S(1)}, bf16[2,208,1024]{2,1,0:T(8,128)(2,1)S(1)}, u32[]{:S(2)}, u32[]{:S(2)}) collective-permute-start(bf16[2,208,1024]{2,1,0:T(8,128)(2,1)S(1)} %get-tuple-element.103), channel_id=1, source_target_pairs={{0,1},{1,0},{2,3},{3,2},{4,5},{5,4},{6,7},{7,6},{8,9},{9,8},{10,11... | collective-permute-start | bytes 2555912 | tf_op jit(solution)/shard_map/ppermute | solution.py:631
  84.8 11.9 %collective-permute-start.23 = (bf16[208,1024]{1,0:T(8,128)(2,1)S(1)}, bf16[208,1024]{1,0:T(8,128)(2,1)S(1)}, u32[]{:S(2)}, u32[]{:S(2)}) collective-permute-start(bf16[208,1024]{1,0:T(8,128)(2,1)S(1)} %fusion.3), channel_id=1, source_target_pairs={{0,2},{1,3},{2,0},{3,1},{4,6},{5,7},{6,4},{7,5},{8,10},{9,11},{10,... | collective-permute-start | bytes 1277960 | tf_op jit(solution)/shard_map/ppermute | solution.py:631
  97.0 18.9 %copy-start.33 = (s32[512]{0:T(512)S(1)}, s32[512]{0:T(512)}, u32[]{:S(2)}) copy-start(s32[512]{0:T(512)} %refs_8_.1) | copy-start | bytes 6148
  97.0 18.9 %copy-start.34 = (s32[512]{0:T(512)S(1)}, s32[512]{0:T(512)}, u32[]{:S(2)}) copy-start(s32[512]{0:T(512)} %slot.3) | copy-start | bytes 6148
  97.0 27.5 %copy-start.44 = (bf16[512,768]{1,0:T(8,128)(2,1)S(1)}, bf16[512,768]{1,0:T(8,128)(2,1)}, u32[]{:S(2)}) copy-start(bf16[512,768]{1,0:T(8,128)(2,1)} %get-tuple-element.109.refs_14_.normed) | copy-start | bytes 2359300
  97.0 27.5 %copy-start.45 = (bf16[768,512]{1,0:T(8,128)(2,1)S(1)}, bf16[768,512]{1,0:T(8,128)(2,1)}, u32[]{:S(2)}) copy-start(bf16[768,512]{1,0:T(8,128)(2,1)} %get-tuple-element.107.refs_10_) | copy-start | bytes 2359300
  99.2 23.9 %collective-permute-start.24 = (bf16[2,192,1024]{2,1,0:T(8,128)(2,1)S(1)}, bf16[2,192,1024]{2,1,0:T(8,128)(2,1)S(1)}, u32[]{:S(2)}, u32[]{:S(2)}) collective-permute-start(bf16[2,192,1024]{2,1,0:T(8,128)(2,1)S(1)} %get-tuple-element.105), channel_id=1, source_target_pairs={{0,1},{1,0},{2,3},{3,2},{4,5},{5,4},{6,7},{7,6},{8,9},{9,8},{10,11... | collective-permute-start | bytes 2359304 | tf_op jit(solution)/shard_map/ppermute | solution.py:631
  99.3 25.2 %copy-start.43 = (f32[3,512,512]{2,1,0:T(8,128)S(1)}, f32[3,512,512]{2,1,0:T(8,128)}, u32[]{:S(2)}) copy-start(f32[3,512,512]{2,1,0:T(8,128)} %get-tuple-element.108.refs_13_.probs) | copy-start | bytes 9437188
  99.4 7.7 %collective-permute-start.35 = (bf16[208,128]{1,0:T(8,128)(2,1)S(1)}, bf16[208,128]{1,0:T(8,128)(2,1)S(1)}, u32[]{:S(2)}, u32[]{:S(2)}) collective-permute-start(bf16[208,128]{1,0:T(8,128)(2,1)S(1)} %get-tuple-element.164), channel_id=1, source_target_pairs={{0,28},{4,24},{8,20},{12,16},{16,12},{20,8},{24,4},{28,0},{1,29},{... | collective-permute-start | bytes 159752 | tf_op jit(solution)/shard_map/ppermute | solution.py:631
  101.5 6.4 %collective-permute-start.34 = (bf16[208,128]{1,0:T(8,128)(2,1)S(1)}, bf16[208,128]{1,0:T(8,128)(2,1)S(1)}, u32[]{:S(2)}, u32[]{:S(2)}) collective-permute-start(bf16[208,128]{1,0:T(8,128)(2,1)S(1)} %get-tuple-element.165), channel_id=1, source_target_pairs={{0,24},{4,28},{8,16},{12,20},{16,8},{20,12},{24,0},{28,4},{1,25},{... | collective-permute-start | bytes 159752 | tf_op jit(solution)/shard_map/ppermute | solution.py:631
  103.6 8.1 %collective-permute-start.33 = (bf16[208,128]{1,0:T(8,128)(2,1)S(1)}, bf16[208,128]{1,0:T(8,128)(2,1)S(1)}, u32[]{:S(2)}, u32[]{:S(2)}) collective-permute-start(bf16[208,128]{1,0:T(8,128)(2,1)S(1)} %get-tuple-element.166), channel_id=1, source_target_pairs={{0,20},{4,16},{8,28},{12,24},{16,4},{20,0},{24,12},{28,8},{1,21},{... | collective-permute-start | bytes 159752 | tf_op jit(solution)/shard_map/ppermute | solution.py:631
  103.6 9.6 %collective-permute-start.32 = (bf16[208,128]{1,0:T(8,128)(2,1)S(1)}, bf16[208,128]{1,0:T(8,128)(2,1)S(1)}, u32[]{:S(2)}, u32[]{:S(2)}) collective-permute-start(bf16[208,128]{1,0:T(8,128)(2,1)S(1)} %get-tuple-element.167), channel_id=1, source_target_pairs={{0,16},{4,20},{8,24},{12,28},{16,0},{20,4},{24,8},{28,12},{1,17},{... | collective-permute-start | bytes 159752 | tf_op jit(solution)/shard_map/ppermute | solution.py:631
  107.1 6.7 %collective-permute-start.31 = (bf16[208,128]{1,0:T(8,128)(2,1)S(1)}, bf16[208,128]{1,0:T(8,128)(2,1)S(1)}, u32[]{:S(2)}, u32[]{:S(2)}) collective-permute-start(bf16[208,128]{1,0:T(8,128)(2,1)S(1)} %get-tuple-element.168), channel_id=1, source_target_pairs={{0,12},{4,8},{8,4},{12,0},{16,28},{20,24},{24,20},{28,16},{1,13},{... | collective-permute-start | bytes 159752 | tf_op jit(solution)/shard_map/ppermute | solution.py:631
  107.8 6.0 %collective-permute-start.30 = (bf16[208,128]{1,0:T(8,128)(2,1)S(1)}, bf16[208,128]{1,0:T(8,128)(2,1)S(1)}, u32[]{:S(2)}, u32[]{:S(2)}) collective-permute-start(bf16[208,128]{1,0:T(8,128)(2,1)S(1)} %get-tuple-element.169), channel_id=1, source_target_pairs={{0,8},{4,12},{8,0},{12,4},{16,24},{20,28},{24,16},{28,20},{1,9},{5... | collective-permute-start | bytes 159752 | tf_op jit(solution)/shard_map/ppermute | solution.py:631
  111.7 4.1 %collective-permute-start.29 = (bf16[208,128]{1,0:T(8,128)(2,1)S(1)}, bf16[208,128]{1,0:T(8,128)(2,1)S(1)}, u32[]{:S(2)}, u32[]{:S(2)}) collective-permute-start(bf16[208,128]{1,0:T(8,128)(2,1)S(1)} %get-tuple-element.170), channel_id=1, source_target_pairs={{0,4},{4,0},{8,12},{12,8},{16,20},{20,16},{24,28},{28,24},{1,5},{5... | collective-permute-start | bytes 159752 | tf_op jit(solution)/shard_map/ppermute | solution.py:631
  117.2 5.9 %collective-permute-start.37 = (bf16[208,512]{1,0:T(8,128)(2,1)S(1)}, bf16[208,512]{1,0:T(8,128)(2,1)S(1)}, u32[]{:S(2)}, u32[]{:S(2)}) collective-permute-start(bf16[208,512]{1,0:T(8,128)(2,1)S(1)} %shard_map.256.refs_1_), channel_id=1, source_target_pairs={{0,2},{1,3},{2,0},{3,1},{4,6},{5,7},{6,4},{7,5},{8,10},{9,11},{10,... | collective-permute-start | bytes 638984 | tf_op jit(solution)/shard_map/ppermute | solution.py:631
  117.7 6.1 %collective-permute-start.36 = (bf16[208,512]{1,0:T(8,128)(2,1)S(1)}, bf16[208,512]{1,0:T(8,128)(2,1)S(1)}, u32[]{:S(2)}, u32[]{:S(2)}) collective-permute-start(bf16[208,512]{1,0:T(8,128)(2,1)S(1)} %shard_map.256.refs_1_), channel_id=1, source_target_pairs={{0,1},{1,0},{2,3},{3,2},{4,5},{5,4},{6,7},{7,6},{8,9},{9,8},{10,11... | collective-permute-start | bytes 638984 | tf_op jit(solution)/shard_map/ppermute | solution.py:631
  123.1 1.5 collective-permute-start.38
  123.2 24.6 %collective-permute-start.25 = (bf16[192,1024]{1,0:T(8,128)(2,1)S(1)}, bf16[192,1024]{1,0:T(8,128)(2,1)S(1)}, u32[]{:S(2)}, u32[]{:S(2)}) collective-permute-start(bf16[192,1024]{1,0:T(8,128)(2,1)S(1)} %fusion.5.refs_15_), channel_id=1, source_target_pairs={{0,2},{1,3},{2,0},{3,1},{4,6},{5,7},{6,4},{7,5},{8,10},{9,11},{10,... | collective-permute-start | bytes 1179656 | tf_op jit(solution)/shard_map/ppermute | solution.py:631
  124.6 18.4 %copy-start.21 = (s32[1024]{0:T(1024)S(1)}, s32[1024]{0:T(1024)}, u32[]{:S(2)}) copy-start(s32[1024]{0:T(1024)} %pad_add_fusion.refs_6_.bucket) | copy-start | bytes 12292
  124.6 18.4 %copy-start.47 = (bf16[512,192]{1,0:T(8,128)(2,1)S(1)}, bf16[512,192]{1,0:T(8,128)(2,1)}, u32[]{:S(2)}) copy-start(bf16[512,192]{1,0:T(8,128)(2,1)} %get-tuple-element.111.query) | copy-start | bytes 589828
  124.6 18.4 %copy-start.48 = (bf16[512,192]{1,0:T(8,128)(2,1)S(1)}, bf16[512,192]{1,0:T(8,128)(2,1)}, u32[]{:S(2)}) copy-start(bf16[512,192]{1,0:T(8,128)(2,1)} %get-tuple-element.112.key) | copy-start | bytes 589828
  124.6 18.4 %copy-start.49 = (bf16[512,192]{1,0:T(8,128)(2,1)S(1)}, bf16[512,192]{1,0:T(8,128)(2,1)}, u32[]{:S(2)}) copy-start(bf16[512,192]{1,0:T(8,128)(2,1)} %get-tuple-element.113.value) | copy-start | bytes 589828
  141.5 9.1 %collective-permute-start.39 = (bf16[192,768]{1,0:T(8,128)(2,1)S(1)}, bf16[192,768]{1,0:T(8,128)(2,1)S(1)}, u32[]{:S(2)}, u32[]{:S(2)}) collective-permute-start(bf16[192,768]{1,0:T(8,128)(2,1)S(1)} %get-tuple-element.121), channel_id=1, source_target_pairs={{0,4},{4,0},{8,12},{12,8},{16,20},{20,16},{24,28},{28,24},{1,5},{5... | collective-permute-start | bytes 884744 | tf_op jit(solution)/shard_map/ppermute | solution.py:631
  148.8 10.3 %collective-permute-start.26 = (bf16[768,128]{1,0:T(8,128)(2,1)}, bf16[768,128]{1,0:T(8,128)(2,1)}, u32[]{:S(2)}, u32[]{:S(2)}) collective-permute-start(bf16[768,128]{1,0:T(8,128)(2,1)} %pad_maximum_fusion.6), channel_id=1, source_target_pairs={{0,4},{4,0},{8,12},{12,8},{16,20},{20,16},{24,28},{28,24},{1,5},{5... | collective-permute-start | bytes 589832 | tf_op jit(solution)/shard_map/ppermute | solution.py:631
  157.6 10.7 %collective-permute-start.50 = (bf16[96,768]{1,0:T(8,128)(2,1)S(1)}, bf16[96,768]{1,0:T(8,128)(2,1)}, u32[]{:S(2)}, u32[]{:S(2)}) collective-permute-start(bf16[96,768]{1,0:T(8,128)(2,1)S(1)} %get-tuple-element.163), channel_id=1, source_target_pairs={{0,8},{4,12},{8,0},{12,4},{16,24},{20,28},{24,16},{28,20},{1,9},{5... | collective-permute-start | bytes 442376 | tf_op jit(solution)/shard_map/ppermute | solution.py:631
  157.6 8.8 %collective-permute-start.42 = (bf16[208,768]{1,0:T(8,128)(2,1)S(1)}, bf16[208,768]{1,0:T(8,128)(2,1)S(1)}, u32[]{:S(2)}, u32[]{:S(2)}) collective-permute-start(bf16[208,768]{1,0:T(8,128)(2,1)S(1)} %copy-done.27), channel_id=1, source_target_pairs={{0,4},{4,0},{8,12},{12,8},{16,20},{20,16},{24,28},{28,24},{1,5},{5... | collective-permute-start | bytes 958472 | tf_op jit(solution)/shard_map/ppermute | solution.py:631
  159.1 25.3 %collective-permute-start.40 = (bf16[2,512,256]{2,1,0:T(8,128)(2,1)S(1)}, bf16[2,512,256]{2,1,0:T(8,128)(2,1)}, u32[]{:S(2)}, u32[]{:S(2)}) collective-permute-start(bf16[2,512,256]{2,1,0:T(8,128)(2,1)S(1)} %get-tuple-element.123), channel_id=1, source_target_pairs={{0,1},{1,0},{2,3},{3,2},{4,5},{5,4},{6,7},{7,6},{8,9},{9,8},{10,11... | collective-permute-start | bytes 1572872 | tf_op jit(solution)/shard_map/ppermute | solution.py:631
  160.7 9.3 %collective-permute-start.27 = (bf16[768,128]{1,0:T(8,128)(2,1)}, bf16[768,128]{1,0:T(8,128)(2,1)}, u32[]{:S(2)}, u32[]{:S(2)}) collective-permute-start(bf16[768,128]{1,0:T(8,128)(2,1)} %pad_maximum_fusion.7), channel_id=1, source_target_pairs={{0,8},{4,12},{8,0},{12,4},{16,24},{20,28},{24,16},{28,20},{1,9},{5... | collective-permute-start | bytes 589832 | tf_op jit(solution)/shard_map/ppermute | solution.py:631
  166.5 8.1 %collective-permute-start.43 = (bf16[112,768]{1,0:T(8,128)(2,1)S(1)}, bf16[112,768]{1,0:T(8,128)(2,1)S(1)}, u32[]{:S(2)}, u32[]{:S(2)}) collective-permute-start(bf16[112,768]{1,0:T(8,128)(2,1)S(1)} %get-tuple-element.127.refs_1_), channel_id=1, source_target_pairs={{0,8},{4,12},{8,0},{12,4},{16,24},{20,28},{24,16},{28,20},{1,9},{5... | collective-permute-start | bytes 516104 | tf_op jit(solution)/shard_map/ppermute | solution.py:631
  169.2 14.1 %collective-permute-start.51 = (bf16[48,768]{1,0:T(8,128)(2,1)S(1)}, bf16[48,768]{1,0:T(8,128)(2,1)}, u32[]{:S(2)}, u32[]{:S(2)}) collective-permute-start(bf16[48,768]{1,0:T(8,128)(2,1)S(1)} %add_convert_fusion.9), channel_id=1, source_target_pairs={{0,16},{4,20},{8,24},{12,28},{16,0},{20,4},{24,8},{28,12},{1,17},{... | collective-permute-start | bytes 221192 | tf_op jit(solution)/shard_map/ppermute | solution.py:631
  171.6 29.0 %collective-permute-start.28 = (bf16[768,128]{1,0:T(8,128)(2,1)}, bf16[768,128]{1,0:T(8,128)(2,1)}, u32[]{:S(2)}, u32[]{:S(2)}) collective-permute-start(bf16[768,128]{1,0:T(8,128)(2,1)} %pad_maximum_fusion.8), channel_id=1, source_target_pairs={{0,16},{4,20},{8,24},{12,28},{16,0},{20,4},{24,8},{28,12},{1,17},{... | collective-permute-start | bytes 589832 | tf_op jit(solution)/shard_map/ppermute | solution.py:631
  174.7 20.3 %collective-permute-start.44 = (bf16[64,768]{1,0:T(8,128)(2,1)S(1)}, bf16[64,768]{1,0:T(8,128)(2,1)S(1)}, u32[]{:S(2)}, u32[]{:S(2)}) collective-permute-start(bf16[64,768]{1,0:T(8,128)(2,1)S(1)} %get-tuple-element.129.refs_1_), channel_id=1, source_target_pairs={{0,16},{4,20},{8,24},{12,28},{16,0},{20,4},{24,8},{28,12},{1,17},{... | collective-permute-start | bytes 294920 | tf_op jit(solution)/shard_map/ppermute | solution.py:631
  184.3 13.8 %collective-permute-start.52 = (bf16[48,768]{1,0:T(8,128)(2,1)S(1)}, bf16[48,768]{1,0:T(8,128)(2,1)S(1)}, u32[]{:S(2)}, u32[]{:S(2)}) collective-permute-start(bf16[48,768]{1,0:T(8,128)(2,1)S(1)} %add_convert_fusion.8), channel_id=1, source_target_pairs={{0,16},{4,20},{8,24},{12,28},{16,0},{20,4},{24,8},{28,12},{1,17},{... | collective-permute-start | bytes 221192 | tf_op jit(solution)/shard_map/ppermute | solution.py:631
  186.3 28.2 %collective-permute-start.41 = (bf16[512,256]{1,0:T(8,128)(2,1)}, bf16[512,256]{1,0:T(8,128)(2,1)S(1)}, u32[]{:S(2)}, u32[]{:S(2)}) collective-permute-start(bf16[512,256]{1,0:T(8,128)(2,1)} %get-tuple-element.160.refs_4_), channel_id=1, source_target_pairs={{0,2},{1,3},{2,0},{3,1},{4,6},{5,7},{6,4},{7,5},{8,10},{9,11},{10,... | collective-permute-start | bytes 786440 | tf_op jit(solution)/shard_map/ppermute | solution.py:631
  195.1 6.4 %collective-permute-start.45 = (f32[8,768]{1,0:T(8,128)S(1)}, f32[8,768]{1,0:T(8,128)S(1)}, u32[]{:S(2)}, u32[]{:S(2)}) collective-permute-start(f32[8,768]{1,0:T(8,128)S(1)} %get-tuple-element.130), channel_id=1, source_target_pairs={{0,1},{1,0},{2,3},{3,2},{4,5},{5,4},{6,7},{7,6},{8,9},{9,8},{10,11... | collective-permute-start | bytes 73736 | tf_op jit(solution)/shard_map/ppermute | solution.py:631
  195.1 7.5 %collective-permute-start.47 = (bf16[48,768]{1,0:T(8,128)(2,1)S(1)}, bf16[48,768]{1,0:T(8,128)(2,1)S(1)}, u32[]{:S(2)}, u32[]{:S(2)}) collective-permute-start(bf16[48,768]{1,0:T(8,128)(2,1)S(1)} %get-tuple-element.131.refs_1_), channel_id=1, source_target_pairs={{0,16},{4,20},{8,24},{12,28},{16,0},{20,4},{24,8},{28,12},{1,17},{... | collective-permute-start | bytes 221192 | tf_op jit(solution)/shard_map/ppermute | solution.py:631
  199.6 8.1 %collective-permute-start.53 = (bf16[96,768]{1,0:T(8,128)(2,1)S(1)}, bf16[96,768]{1,0:T(8,128)(2,1)S(1)}, u32[]{:S(2)}, u32[]{:S(2)}) collective-permute-start(bf16[96,768]{1,0:T(8,128)(2,1)S(1)} %pad_maximum_fusion.9.mine), channel_id=1, source_target_pairs={{0,8},{4,12},{8,0},{12,4},{16,24},{20,28},{24,16},{28,20},{1,9},{5... | collective-permute-start | bytes 442376 | tf_op jit(solution)/shard_map/ppermute | solution.py:631
  201.5 6.2 %collective-permute-start.46 = (f32[8,768]{1,0:T(8,128)S(1)}, f32[8,768]{1,0:T(8,128)S(1)}, u32[]{:S(2)}, u32[]{:S(2)}) collective-permute-start(f32[8,768]{1,0:T(8,128)S(1)} %add.59), channel_id=1, source_target_pairs={{0,2},{1,3},{2,0},{3,1},{4,6},{5,7},{6,4},{7,5},{8,10},{9,11},{10,... | collective-permute-start | bytes 73736 | tf_op jit(solution)/shard_map/ppermute | solution.py:631
  202.7 9.6 %collective-permute-start.48 = (bf16[96,768]{1,0:T(8,128)(2,1)S(1)}, bf16[96,768]{1,0:T(8,128)(2,1)S(1)}, u32[]{:S(2)}, u32[]{:S(2)}) collective-permute-start(bf16[96,768]{1,0:T(8,128)(2,1)S(1)} %constant_dynamic-update-slice_fusion.refs_1_.mine), channel_id=1, source_target_pairs={{0,8},{4,12},{8,0},{12,4},{16,24},{20,28},{24,16},{28,20},{1,9},{5... | collective-permute-start | bytes 442376 | tf_op jit(solution)/shard_map/ppermute | solution.py:631
  210.1 10.3 %collective-permute-start.54 = (bf16[192,768]{1,0:T(8,128)(2,1)}, bf16[192,768]{1,0:T(8,128)(2,1)S(1)}, u32[]{:S(2)}, u32[]{:S(2)}) collective-permute-start(bf16[192,768]{1,0:T(8,128)(2,1)} %pad_maximum_fusion.2), channel_id=1, source_target_pairs={{0,4},{4,0},{8,12},{12,8},{16,20},{20,16},{24,28},{28,24},{1,5},{5... | collective-permute-start | bytes 884744 | tf_op jit(solution)/shard_map/ppermute | solution.py:631
  213.9 11.4 %collective-permute-start.49 = (bf16[192,768]{1,0:T(8,128)(2,1)}, bf16[192,768]{1,0:T(8,128)(2,1)S(1)}, u32[]{:S(2)}, u32[]{:S(2)}) collective-permute-start(bf16[192,768]{1,0:T(8,128)(2,1)} %pad_maximum_fusion.1), channel_id=1, source_target_pairs={{0,4},{4,0},{8,12},{12,8},{16,20},{20,16},{24,28},{28,24},{1,5},{5... | collective-permute-start | bytes 884744 | tf_op jit(solution)/shard_map/ppermute | solution.py:631
  (50 other events, 223.1 us)
